TPU v7x, 256 devices: a whole 4x4x8 slice. The times are simulated.
256 devices in a mesh: lon: 8 (over x, core), lat: 8 (over z), mem: 4 (over y).
Axes of the slice: x: 4, y: 4, z: 8, core: 2. Of those that a mesh axis runs over, the one named last changes fastest.
Arguments:
- control: float32 [640, 64, 1024], P('mem', 'lat', 'lon'), may hold values from -6 to 6
- residual: float32 [640, 64, 1024], P('mem', 'lat', 'lon'), may hold values from -6 to 6
- direction: float32 [640, 64, 1024], P('mem', 'lat', 'lon'), may hold values from -6 to 6
- members: bfloat16 [80, 32, 64, 1024], P('mem', None, 'lat', 'lon'), may hold values from -0.625 to 0.625
- vert_modes: float32 [8, 32], replicated, may hold values from -2 to 2
- eig_count: int32 [80], P('mem'), may hold values from 1 to 8, as said below
- lon_decay: float32 [64], P('lat'), may hold values from 0.00048828125 to 0.03125
- lat_decay: float32 [1024], P('lon'), may hold values from 0.0078125 to 0.5
- obs_weight: float32 [32, 64, 1024], P(None, 'lat', 'lon'), may hold values from 0.25 to 4
Outputs:
- new_control: float32 [640, 64, 1024], P('mem', 'lat', 'lon')
- new_residual: float32 [640, 64, 1024], P('mem', 'lat', 'lon')
- new_direction: float32 [640, 64, 1024], P('mem', 'lat', 'lon')
Inputs may be any that keep to these rules, and one draw needn't show every extreme that they name: Member m uses its first eig_count[m] vertical modes; some member uses all 8.
All inputs are finite; a program needn't handle non-finite values.
Results may differ from a plain program's by a relative error of at most 0.0009.
Values sent between devices are 32-bit elements; how exact they have to be, the bound alone decides.
A program may use at most 64 MiB of HBM per device.

v0:
```python
import jax
import jax.numpy as jnp
from jax import lax
from jax.sharding import PartitionSpec as P

highest = lax.Precision.HIGHEST


def carried_in(x, axis, combine, identity, reverse):
    count, mine = (lax.axis_size(axis), lax.axis_index(axis))
    everything = jax.tree.map(lambda part: lax.all_gather(part, axis), x)
    start = jax.tree.map(
        lambda part, zero: jnp.broadcast_to(jnp.asarray(zero, part.dtype), part.shape), x, identity
    )

    def step(k, before):
        at = count - 1 - k if reverse else k
        reached = at > mine if reverse else at < mine
        new = combine(before, jax.tree.map(lambda part: part[at], everything))
        return jax.tree.map(lambda a, b: jnp.where(reached, a, b), new, before)

    return lax.fori_loop(0, count, step, start)


def broadcast(x, axis, root):
    mine = lax.axis_index(axis) == root
    return lax.psum(jnp.where(mine, x, jnp.zeros_like(x)), axis)


def binomial(offset, degree):
    result = jnp.ones_like(offset)
    for factor in range(degree):
        result = result * (offset + factor + 1.0) / (factor + 1.0)
    return result


def transition(decays, length):
    leakage = 1.0 - jnp.exp(-decays)
    closing = jnp.exp(-length * decays)
    zeroes = jnp.zeros_like(decays)
    matrix_rows = []
    for target in range(4):
        entries = []
        for source in range(4):
            if source <= target:
                spread = target - source
                entries.append(
                    binomial(jnp.full_like(decays, length - 1.0), spread)
                    * leakage**spread
                    * closing
                )
            else:
                entries.append(zeroes)
        matrix_rows.append(jnp.stack(entries))
    return jnp.stack(matrix_rows)


def periodic_start(matrix, totals):
    solved = []
    for target in range(4):
        running = totals[target]
        for source in range(target):
            running = running + matrix[target, source] * solved[source]
        solved.append(running / (1.0 - matrix[target, target]))
    return jnp.stack(solved)


def travel_places(length, backward):
    places = jnp.arange(length).astype(jnp.float32)
    if backward:
        places = length - 1.0 - places
    return places


def kernel_table(decays, length, backward):
    leakage = 1.0 - jnp.exp(-decays)
    scaling = 2.5 / jnp.sqrt(leakage)
    places = travel_places(length, backward)
    offsets = places[:, None] - places[None, :]
    lagged = jnp.maximum(offsets, 0.0)
    shaped = binomial(lagged, 3)[None] * jnp.exp(-lagged[None] * decays[:, None, None])
    return jnp.where(offsets[None] >= 0.0, (leakage**4 * scaling)[:, None, None] * shaped, 0.0)


def edge_tables(decays, length, backward):
    leakage = 1.0 - jnp.exp(-decays)
    scaling = 2.5 / jnp.sqrt(leakage)
    places = travel_places(length, backward)
    remain = length - 1.0 - places
    finals = jnp.stack(
        [
            (leakage ** (section_index + 1) * scaling)[:, None]
            * binomial(remain, section_index)[None, :]
            * jnp.exp(-remain[None, :] * decays[:, None])
            for section_index in range(4)
        ]
    )
    entering = jnp.stack(
        [
            (leakage ** (3 - section_index))[:, None]
            * binomial(places, 3 - section_index)[None, :]
            * jnp.exp(-(places[None, :] + 1.0) * decays[:, None])
            for section_index in range(4)
        ],
        axis=2,
    )
    return (finals, entering, transition(decays, length))


def compose(earlier, later):
    matrix = jnp.einsum("kir,ijr->kjr", later[0], earlier[0], precision=highest)
    carried = jnp.einsum("kjr,jfr->kfr", later[0], earlier[1], precision=highest) + later[1]
    return (matrix, carried)


def neutral_of(matrix, carried):
    return (
        jnp.broadcast_to(jnp.eye(4, dtype=jnp.float32)[:, :, None], matrix.shape),
        jnp.zeros_like(carried),
    )


def lon_filter(fields, decays, backward):
    length = fields.shape[2]
    kernel = kernel_table(decays, length, backward)
    finals, entering, matrix = edge_tables(decays, length, backward)
    inside = jnp.einsum("aij,kaj->kai", kernel, fields, precision=highest)
    carried = jnp.einsum("saj,kaj->ska", finals, fields, precision=highest)
    own_block = (matrix, carried)
    neutral = neutral_of(matrix, carried)
    devices_lon = lax.axis_size("lon")
    cycle_matrix = transition(decays, length * devices_lon)
    before = carried_in(own_block, "lon", compose, neutral, backward)
    through = compose(before, own_block)
    root_index = 0 if backward else devices_lon - 1
    cycle_states = broadcast(through[1], "lon", root_index)
    anchor = periodic_start(cycle_matrix, cycle_states)
    incoming = jnp.einsum("kjr,jfr->kfr", before[0], anchor, precision=highest) + before[1]
    return inside + jnp.einsum("ais,ska->kai", entering, incoming, precision=highest)


def lat_filter(fields, decays, backward):
    length = fields.shape[1]
    kernel = kernel_table(decays, length, backward)
    finals, entering, matrix = edge_tables(decays, length, backward)
    inside = jnp.einsum("cij,kjc->kic", kernel, fields, precision=highest)
    carried = jnp.einsum("scj,kjc->skc", finals, fields, precision=highest)
    own_block = (matrix, carried)
    before = carried_in(own_block, "lat", compose, neutral_of(matrix, carried), backward)
    return inside + jnp.einsum("cis,skc->kic", entering, before[1], precision=highest)


def body(
    control, residual, direction, members, vert_modes, eig_count, lon_decay, lat_decay, obs_weight
):
    mode_count = vert_modes.shape[0]
    member_count = eig_count.shape[0]
    lat_cells = direction.shape[1]
    lon_cells = direction.shape[2]
    active = (jnp.arange(mode_count)[None, :] < eig_count[:, None]).astype(jnp.float32).reshape(-1)
    norm_old = lax.psum(jnp.sum(residual * residual), ("lon", "lat", "mem"))
    smooth = (
        lat_filter(lon_filter(direction, lon_decay, False), lat_decay, False)
        * active[:, None, None]
    )
    weights = smooth.reshape(member_count, mode_count, lat_cells, lon_cells)
    profile = jnp.einsum("el,meyx->mlyx", vert_modes, weights, precision=highest)
    partial_value = jnp.sum(members.astype(jnp.float32) * profile, axis=0)
    increment = lax.psum(partial_value, "mem")
    weighted = obs_weight * increment
    projected = jnp.einsum(
        "el,mlyx->meyx", vert_modes, members.astype(jnp.float32) * weighted[None], precision=highest
    )
    gradient = (
        projected.reshape(member_count * mode_count, lat_cells, lon_cells) * active[:, None, None]
    )
    hessian = direction + lon_filter(lat_filter(gradient, lat_decay, True), lon_decay, True)
    curvature = lax.psum(jnp.sum(direction * hessian), ("lon", "lat", "mem"))
    step_size = norm_old / curvature
    new_control = control + step_size * direction
    new_residual = residual - step_size * hessian
    norm_new = lax.psum(jnp.sum(new_residual * new_residual), ("lon", "lat", "mem"))
    new_direction = new_residual + norm_new / norm_old * direction
    return (new_control, new_residual, new_direction)


def solution(mesh):
    placed = (
        P("mem", "lat", "lon"),
        P("mem", "lat", "lon"),
        P("mem", "lat", "lon"),
        P("mem", None, "lat", "lon"),
        P(),
        P("mem"),
        P("lat"),
        P("lon"),
        P(None, "lat", "lon"),
    )
    return jax.shard_map(
        body,
        mesh=mesh,
        in_specs=placed,
        out_specs=(P("mem", "lat", "lon"), P("mem", "lat", "lon"), P("mem", "lat", "lon")),
        check_vma=False,
    )
```

profile of v0, /device:TPU:1, one launch (start us, length us, event | category | flops | bytes accessed | tf_op | source)
XLA Modules:
  0.0 497.2 jit_solution(14770768469935394832)
XLA Ops:
  9.8 2.2 fusion.69
  12.0 15.9 %all-gather.1 = f32[32,160,8]{1,2,0:T(8,128)S(1)} all-gather(f32[4,160,8]{1,2,0:T(8,128)S(1)} %bitcast.257), channel_id=3, replica_groups=mesh['lon'=8,'lat'=8,'mem'=4] {'lon'}, dimensions={0}, use_global_device_ids=true | all-gather | bytes 184320 | tf_op jit(solution)/shard_map/all_gather | solution.py:11
  28.6 12.7 %all-gather = f32[32,4,8]{2,1,0:T(4,128)S(1)} all-gather(f32[4,4,8]{2,1,0:T(4,128)S(1)} %copy.182), channel_id=2, replica_groups=mesh['lon'=8,'lat'=8,'mem'=4] {'lon'}, dimensions={0}, use_global_device_ids=true | all-gather | bytes 4608 | tf_op jit(solution)/shard_map/all_gather | solution.py:11
  41.3 4.4 while.64
  45.9 21.0 %psum.43 = f32[4,160,8]{1,2,0:T(8,128)S(1)} all-reduce(f32[4,160,8]{1,2,0:T(8,128)S(1)} %fusion.113), channel_id=1, replica_groups=mesh['lon'=8,'lat'=8,'mem'=4] {'lon'}, use_global_device_ids=true, to_apply=%region_4.5 | all-reduce | flops 5120 | bytes 40960 | tf_op jit(solution)/shard_map/psum | solution.py:27
  68.1 1.3 convolution_bitcast_fusion.7
  69.4 1.4 fusion.41
  72.3 1.0 convolution_bitcast_fusion.9
  74.4 22.6 %all-gather.2 = f32[32,4,128]{2,1,0:T(4,128)S(1)} all-gather(f32[4,4,128]{2,1,0:T(4,128)S(1)} %pad_maximum_fusion.11), channel_id=4, replica_groups=mesh['lon'=8,'lat'=8,'mem'=4] {'lat'}, dimensions={0}, use_global_device_ids=true | all-gather | bytes 73728 | tf_op jit(solution)/shard_map/all_gather | solution.py:11
  97.1 1.7 copy.194
  100.6 2.2 fusion.58
  102.8 14.6 %all-gather.9.cloned.1.call-done = f32[32,160,128]{2,1,0:T(8,128)} async-done(((f32[4,160,128]{2,1,0:T(8,128)}), f32[32,160,128]{2,1,0:T(8,128)}) %all-gather.9.cloned.1.call-update) | async-done | bytes 2621456 | tf_op jit(solution)/shard_map/all_gather | solution.py:11
  117.4 28.1 %while.65 = (s32[]{:T(128)}, f32[4,160,128]{1,0,2:T(4,128)S(1)}, s32[]{:T(128)}, f32[8,4,4,128]{2,1,3,0:T(4,128)}, f32[8,4,160,128]{3,2,1,0:T(8,128)}, /*index=5*/s32[]{:T(128)}, s32[]{:T(128)}) while((s32[]{:T(128)}, f32[4,160,128]{1,0,2:T(4,128)S(1)}, s32[]{:T(128)}, f32[8,4,4,128]{2,1,3,0:T(4,128)}, ...), condition=%wide.region_6.7_spmd.clone, body=%wide.region_5.6_spmd.clone.sunk | while | flops 4259844 | bytes 4130915 | solution.py:22
  117.4 1.1 constant_dynamic-slice_fusion.9
  118.7 2.2 fusion.243
  120.9 1.0 constant_dynamic-slice_fusion.9
  122.2 2.2 fusion.243
  124.4 1.0 constant_dynamic-slice_fusion.9
  125.7 2.2 fusion.243
  127.9 1.0 constant_dynamic-slice_fusion.9
  129.2 2.2 fusion.243
  131.4 1.0 constant_dynamic-slice_fusion.9
  132.7 2.2 fusion.243
  134.9 1.0 constant_dynamic-slice_fusion.9
  136.2 2.2 fusion.243
  139.7 2.2 fusion.243
  143.2 2.2 fusion.243
  145.5 2.0 fusion.36
  147.5 1.4 copy.197
  148.8 4.5 fusion.32
  154.5 44.9 %all-reduce.3.cloned.1.call-done = f32[32,8,128]{2,0,1:T(8,128)} async-done(((f32[32,8,128]{2,0,1:T(8,128)}), f32[32,8,128]{2,0,1:T(8,128)}) %all-reduce.3.cloned.1.call-update) | async-done | bytes 131088 | tf_op jit(solution)/shard_map/psum | solution.py:169
  200.3 1.6 fusion.38
  202.9 2.0 convolution_bitcast_fusion.8
  208.0 2.2 fusion.52
  210.1 37.8 %all-gather.11.cloned.1.call-done = f32[32,160,128]{2,1,0:T(8,128)} async-done(((f32[4,160,128]{2,1,0:T(8,128)}), f32[32,160,128]{2,1,0:T(8,128)}) %all-gather.11.cloned.1.call-update) | async-done | bytes 2621456 | tf_op jit(solution)/shard_map/all_gather | solution.py:11
  247.9 28.2 %while.66 = (s32[]{:T(128)}, f32[4,160,128]{1,0,2:T(4,128)S(1)}, s32[]{:T(128)}, f32[8,4,4,128]{2,1,3,0:T(4,128)}, f32[8,4,160,128]{3,2,1,0:T(8,128)}, /*index=5*/s32[]{:T(128)}, s32[]{:T(128)}, s32[]{:T(128)}, s32[]{:T(128)}) while((s32[]{:T(128)}, f32[4,160,128]{1,0,2:T(4,128)S(1)}, s32[]{:T(128)}, ...), condition=%wide.region_10.11_spmd.clone, body=%wide.region_9.10_spmd.clone.sunk | while | flops 4259848 | bytes 4130977 | solution.py:22
  247.9 1.1 constant_dynamic-slice_fusion.10
  249.3 2.2 fusion.246
  251.5 1.0 constant_dynamic-slice_fusion.10
  252.8 2.2 fusion.246
  255.0 1.0 constant_dynamic-slice_fusion.10
  256.3 2.2 fusion.246
  258.5 1.0 constant_dynamic-slice_fusion.10
  259.8 2.2 fusion.246
  262.0 1.0 constant_dynamic-slice_fusion.10
  263.3 2.2 fusion.246
  265.6 1.0 constant_dynamic-slice_fusion.10
  266.9 2.2 fusion.246
  269.1 1.0 constant_dynamic-slice_fusion.10
  270.4 2.2 fusion.246
  272.6 1.0 constant_dynamic-slice_fusion.10
  273.9 2.2 fusion.246
  276.1 2.2 fusion.34
  278.9 1.1 fusion.117
  280.1 16.6 %all-gather.5 = f32[32,160,8]{1,2,0:T(8,128)S(1)} all-gather(f32[4,160,8]{1,2,0:T(8,128)S(1)} %bitcast.258), channel_id=7, replica_groups=mesh['lon'=8,'lat'=8,'mem'=4] {'lon'}, dimensions={0}, use_global_device_ids=true | all-gather | bytes 184320 | tf_op jit(solution)/shard_map/all_gather | solution.py:11
  296.7 10.0 %while.67 = (s32[]{:T(128)}, f32[4,4,8]{1,0,2:T(4,128)S(1)}, f32[4,160,8]{1,0,2:T(4,128)S(1)}, s32[]{:T(128)}, f32[8,4,4,8]{3,2,1,0:T(4,128)}, /*index=5*/f32[8,...) while((s32[]{:T(128)}, f32[4,4,8]{1,0,2:T(4,128)S(1)}, ...), condition=%wide.region_12.13_spmd.clone, body=%wide.region_11.12_spmd.clone.sunk | while | flops 272520 | bytes 148656 | solution.py:22
  307.0 22.4 %psum.45 = f32[4,160,8]{1,2,0:T(8,128)S(1)} all-reduce(f32[4,160,8]{1,2,0:T(8,128)S(1)} %fusion.112), channel_id=1, replica_groups=mesh['lon'=8,'lat'=8,'mem'=4] {'lon'}, use_global_device_ids=true, to_apply=%region_13.14 | all-reduce | flops 5120 | bytes 40960 | tf_op jit(solution)/shard_map/psum | solution.py:27
  329.8 1.3 fusion.46
  331.1 2.0 multiply_reduce_fusion.1
  333.1 77.8 %all-reduce = (f32[]{:T(128)}, f32[]{:T(128)}) all-reduce(f32[]{:T(128)} %multiply_reduce_fusion.2, f32[]{:T(128)} %get-tuple-element.855), channel_id=1, replica_groups=mesh['lon'=8,'lat'=8,'mem'=4] {'lon','lat','mem'}, use_global_device_ids=true, to_apply=%region_1.0 | all-reduce | flops 2 | bytes 16 | tf_op jit(solution)/shard_map/psum | solution.py:161
  413.1 72.4 %psum.47 = f32[]{:T(128)} all-reduce(f32[]{:T(128)} %get-tuple-element.749), channel_id=1, replica_groups=mesh['lon'=8,'lat'=8,'mem'=4] {'lon','lat','mem'}, use_global_device_ids=true, to_apply=%region_17.18 | all-reduce | flops 1 | bytes 8 | tf_op jit(solution)/shard_map/psum | solution.py:182
  486.8 1.2 copy.223
  488.3 1.2 copy.222
  489.5 1.2 copy.224
  (349 shorter events, 36.6 us)
Async XLA Ops:
  7.2 141.7 %copy-start = (f32[8,32]{1,0:T(8,128)S(1)}, f32[8,32]{1,0:T(8,128)}, u32[]{:S(2)}) copy-start(f32[8,32]{1,0:T(8,128)} %param.21) | copy-start | bytes 3076
  7.2 60.2 %copy-start.20 = (f32[8]{0:T(128)S(1)}, f32[8]{0:T(128)}, u32[]{:S(2)}) copy-start(f32[8]{0:T(128)} %param.23) | copy-start | bytes 100
  7.2 62.2 %copy-start.1 = (f32[160,8,128]{2,1,0:T(8,128)S(1)}, f32[160,8,128]{2,1,0:T(8,128)}, u32[]{:S(2)}) copy-start(f32[160,8,128]{2,1,0:T(8,128)} %param.19) | copy-start | bytes 1966084
  7.2 110.1 %all-gather.9.cloned.1.call-start = ((), (), s32[]{:S(2)}) async-start(), calls=%async_computation.1 | async-start | bytes 2949120 | tf_op jit(solution)/shard_map/all_gather | solution.py:11
  7.4 62.0 %copy-start.16 = (f32[4,4]{1,0:T(4,128)}, f32[4,4]{1,0:T(4,128)S(1)}, u32[]{:S(2)}) copy-start(f32[4,4]{1,0:T(4,128)S(1)} %fusion.166) | copy-start | bytes 196
  8.4 62.4 %copy-start.25 = (f32[8]{0:T(128)}, f32[8]{0:T(128)S(1)}, u32[]{:S(2)}) copy-start(f32[8]{0:T(128)S(1)} %get-tuple-element.842) | copy-start | bytes 100
  28.4 41.0 %copy-start.14 = (f32[1,4,8]{1,0,2:T(1,128)}, f32[1,4,8]{1,0,2:T(1,128)S(1)}, u32[]{:S(2)}) copy-start(f32[1,4,8]{1,0,2:T(1,128)S(1)} %copy.181) | copy-start | bytes 388
  45.7 23.7 %copy-start.8 = (f32[8,4,4,8]{3,2,1,0:T(4,128)}, f32[8,4,4,8]{3,2,1,0:T(4,128)S(1)}, u32[]{:S(2)}) copy-start(f32[8,4,4,8]{3,2,1,0:T(4,128)S(1)} %get-tuple-element.1117) | copy-start | bytes 12292
  45.7 25.6 %copy-start.18 = (f32[128]{0:T(128)S(1)}, f32[128]{0:T(128)}, u32[]{:S(2)}) copy-start(f32[128]{0:T(128)} %param.24) | copy-start | bytes 1540
  67.0 5.1 %copy-start.27 = (f32[8]{0:T(128)}, f32[8]{0:T(128)S(1)}, u32[]{:S(2)}) copy-start(f32[8]{0:T(128)S(1)} %get-tuple-element.768) | copy-start | bytes 100
  67.0 5.1 %copy-start.29 = (f32[8]{0:T(128)}, f32[8]{0:T(128)S(1)}, u32[]{:S(2)}) copy-start(f32[8]{0:T(128)S(1)} %get-tuple-element.769) | copy-start | bytes 100
  67.0 5.0 %copy-start.31 = (f32[8]{0:T(128)}, f32[8]{0:T(128)S(1)}, u32[]{:S(2)}) copy-start(f32[8]{0:T(128)S(1)} %get-tuple-element.770) | copy-start | bytes 100
  67.0 5.0 %copy-start.33 = (f32[8]{0:T(128)}, f32[8]{0:T(128)S(1)}, u32[]{:S(2)}) copy-start(f32[8]{0:T(128)S(1)} %get-tuple-element.771) | copy-start | bytes 100
  67.0 5.0 %copy-start.35 = (f32[8]{0:T(128)}, f32[8]{0:T(128)S(1)}, u32[]{:S(2)}) copy-start(f32[8]{0:T(128)S(1)} %get-tuple-element.857) | copy-start | bytes 100
  67.0 5.0 %copy-start.37 = (f32[8]{0:T(128)}, f32[8]{0:T(128)S(1)}, u32[]{:S(2)}) copy-start(f32[8]{0:T(128)S(1)} %get-tuple-element.858) | copy-start | bytes 100
  67.0 5.0 %copy-start.39 = (f32[8]{0:T(128)}, f32[8]{0:T(128)S(1)}, u32[]{:S(2)}) copy-start(f32[8]{0:T(128)S(1)} %get-tuple-element.859) | copy-start | bytes 100
  67.1 5.0 %copy-start.41 = (f32[8]{0:T(128)}, f32[8]{0:T(128)S(1)}, u32[]{:S(2)}) copy-start(f32[8]{0:T(128)S(1)} %get-tuple-element.763) | copy-start | bytes 100
  67.1 5.0 %copy-start.43 = (f32[8]{0:T(128)}, f32[8]{0:T(128)S(1)}, u32[]{:S(2)}) copy-start(f32[8]{0:T(128)S(1)} %get-tuple-element.764) | copy-start | bytes 100
  67.1 5.0 %copy-start.45 = (f32[8]{0:T(128)}, f32[8]{0:T(128)S(1)}, u32[]{:S(2)}) copy-start(f32[8]{0:T(128)S(1)} %get-tuple-element.860) | copy-start | bytes 100
  71.3 29.3 %copy-start.23 = (f32[128]{0:T(128)}, f32[128]{0:T(128)S(1)}, u32[]{:S(2)}) copy-start(f32[128]{0:T(128)S(1)} %get-tuple-element.835) | copy-start | bytes 1540
  72.3 27.4 %copy-start.47 = (s32[20]{0:T(128)S(1)}, s32[20]{0:T(128)}, u32[]{:S(2)}) copy-start(s32[20]{0:T(128)} %param.22) | copy-start | bytes 244
  74.3 125.1 %all-reduce.3.cloned.1.call-start = ((), (), s32[]{:S(2)}) async-start(), calls=%async_computation | async-start | bytes 262144 | tf_op jit(solution)/shard_map/psum | solution.py:169
  117.3 28.1 %copy-start.2 = (f32[128,160,8]{1,2,0:T(8,128)S(1)}, f32[128,160,8]{1,2,0:T(8,128)}, u32[]{:S(2)}) copy-start(f32[128,160,8]{1,2,0:T(8,128)} %fusion.58) | copy-start | bytes 1966084
  147.4 6.2 %copy-start.12 = (f32[4,128,8]{1,2,0:T(8,128)S(1)}, f32[4,128,8]{1,2,0:T(8,128)}, u32[]{:S(2)}) copy-start(f32[4,128,8]{1,2,0:T(8,128)} %get-tuple-element.866) | copy-start | bytes 49156
  147.4 51.9 %copy-start.9 = (f32[32,8,128]{2,1,0:T(8,128)S(1)}, f32[32,8,128]{2,1,0:T(8,128)}, u32[]{:S(2)}) copy-start(f32[32,8,128]{2,1,0:T(8,128)} %param.25) | copy-start | bytes 393220
  147.5 52.9 %copy-start.6 = (bf16[20,32,8,128]{3,2,1,0:T(8,128)(2,1)S(1)}, bf16[20,32,8,128]{3,2,1,0:T(8,128)(2,1)}, u32[]{:S(2)}) copy-start(bf16[20,32,8,128]{3,2,1,0:T(8,128)(2,1)} %param.20) | copy-start | bytes 3932164
  153.4 48.7 %copy-start.22 = (f32[160]{0:T(256)S(1)}, f32[160]{0:T(256)}, u32[]{:S(2)}) copy-start(f32[160]{0:T(256)} %reshape.3255) | copy-start | bytes 1924
  153.4 94.5 %all-gather.11.cloned.1.call-start = ((), (), s32[]{:S(2)}) async-start(), calls=%async_computation.2 | async-start | bytes 2949120 | tf_op jit(solution)/shard_map/all_gather | solution.py:11
  202.3 4.4 copy-start.4
  202.9 3.0 copy-start.13
  202.9 5.1 %copy-start.19 = (f32[128]{0:T(128)S(1)}, f32[128]{0:T(128)}, u32[]{:S(2)}) copy-start(f32[128]{0:T(128)} %param.24) | copy-start | bytes 1540
  202.9 5.1 %copy-start.24 = (f32[128]{0:T(128)S(1)}, f32[128]{0:T(128)}, u32[]{:S(2)}) copy-start(f32[128]{0:T(128)} %copy-done.23) | copy-start | bytes 1540
  247.9 28.2 %copy-start.3 = (f32[128,160,8]{1,2,0:T(8,128)S(1)}, f32[128,160,8]{1,2,0:T(8,128)}, u32[]{:S(2)}) copy-start(f32[128,160,8]{1,2,0:T(8,128)} %fusion.52) | copy-start | bytes 1966084
  276.1 2.8 copy-start.11
  276.1 20.6 %copy-start.17 = (f32[4,4]{1,0:T(4,128)S(1)}, f32[4,4]{1,0:T(4,128)}, u32[]{:S(2)}) copy-start(f32[4,4]{1,0:T(4,128)} %copy-done.16) | copy-start | bytes 196
  278.3 28.4 %copy-start.15 = (f32[1,4,8]{1,0,2:T(1,128)S(1)}, f32[1,4,8]{1,0,2:T(1,128)}, u32[]{:S(2)}) copy-start(f32[1,4,8]{1,0,2:T(1,128)} %copy-done.14) | copy-start | bytes 388
  278.3 51.1 %copy-start.28 = (f32[8]{0:T(128)S(1)}, f32[8]{0:T(128)}, u32[]{:S(2)}) copy-start(f32[8]{0:T(128)} %copy-done.27) | copy-start | bytes 100
  278.3 51.1 %copy-start.30 = (f32[8]{0:T(128)S(1)}, f32[8]{0:T(128)}, u32[]{:S(2)}) copy-start(f32[8]{0:T(128)} %copy-done.29) | copy-start | bytes 100
  278.4 51.1 %copy-start.32 = (f32[8]{0:T(128)S(1)}, f32[8]{0:T(128)}, u32[]{:S(2)}) copy-start(f32[8]{0:T(128)} %copy-done.31) | copy-start | bytes 100
  278.4 51.1 %copy-start.34 = (f32[8]{0:T(128)S(1)}, f32[8]{0:T(128)}, u32[]{:S(2)}) copy-start(f32[8]{0:T(128)} %copy-done.33) | copy-start | bytes 100
  278.4 51.1 %copy-start.36 = (f32[8]{0:T(128)S(1)}, f32[8]{0:T(128)}, u32[]{:S(2)}) copy-start(f32[8]{0:T(128)} %copy-done.35) | copy-start | bytes 100
  278.4 51.1 %copy-start.38 = (f32[8]{0:T(128)S(1)}, f32[8]{0:T(128)}, u32[]{:S(2)}) copy-start(f32[8]{0:T(128)} %copy-done.37) | copy-start | bytes 100
  278.4 51.1 %copy-start.40 = (f32[8]{0:T(128)S(1)}, f32[8]{0:T(128)}, u32[]{:S(2)}) copy-start(f32[8]{0:T(128)} %copy-done.39) | copy-start | bytes 100
  278.4 51.1 %copy-start.42 = (f32[8]{0:T(128)S(1)}, f32[8]{0:T(128)}, u32[]{:S(2)}) copy-start(f32[8]{0:T(128)} %copy-done.41) | copy-start | bytes 100
  278.4 51.1 %copy-start.44 = (f32[8]{0:T(128)S(1)}, f32[8]{0:T(128)}, u32[]{:S(2)}) copy-start(f32[8]{0:T(128)} %copy-done.43) | copy-start | bytes 100
  278.4 51.1 %copy-start.46 = (f32[8]{0:T(128)S(1)}, f32[8]{0:T(128)}, u32[]{:S(2)}) copy-start(f32[8]{0:T(128)} %copy-done.45) | copy-start | bytes 100
  278.4 51.4 %copy-start.21 = (f32[8]{0:T(128)S(1)}, f32[8]{0:T(128)}, u32[]{:S(2)}) copy-start(f32[8]{0:T(128)} %param.23) | copy-start | bytes 100
  278.4 51.4 %copy-start.26 = (f32[8]{0:T(128)S(1)}, f32[8]{0:T(128)}, u32[]{:S(2)}) copy-start(f32[8]{0:T(128)} %copy-done.25) | copy-start | bytes 100
  278.9 52.2 %copy-start.10 = (f32[8,128,4]{1,0,2:T(8,128)S(1)}, f32[8,128,4]{1,0,2:T(8,128)}, u32[]{:S(2)}) copy-start(f32[8,128,4]{1,0,2:T(8,128)} %get-tuple-element.864) | copy-start | bytes 49156
  296.7 115.6 %copy-start.5 = (f32[160,8,128]{2,1,0:T(8,128)S(1)}, f32[160,8,128]{2,1,0:T(8,128)}, u32[]{:S(2)}) copy-start(f32[160,8,128]{2,1,0:T(8,128)} %param.18) | copy-start | bytes 1966084
  331.1 156.9 %copy-start.7 = (f32[160,8,128]{2,1,0:T(8,128)S(1)}, f32[160,8,128]{2,1,0:T(8,128)}, u32[]{:S(2)}) copy-start(f32[160,8,128]{2,1,0:T(8,128)} %param.17) | copy-start | bytes 1966084
Sparse Core Ops, SparseCore 0:
  74.4 42.8 all-gather.8
  153.5 45.8 all-reduce.2
  206.0 41.8 all-gather.10
where the time goes:
time: 499 us; the launch traced here: 497 us
  blocking collectives  261 us (52%)
  waiting for transfers between devices  97.3 us (19%)
  matrix products  68.8 us (14%)
  local copies, waits for them, and re-layouts  41.7 us (8%)
  between operations  17.5 us (4%)
  other arithmetic  8.56 us (2%)
    psum x1, blocking collectives, body(): norm_old = lax.psum(jnp.sum(residual * residual), ('lon', 'lat', 'mem'))  77.8 us
    psum x1, blocking collectives, body(): lax.psum(jnp.sum(new_residual * new_residual), ('lon', 'lat', 'mem'))  72.4 us
    all_gather x4, blocking collectives, carried_in(): everything = jax.tree.map(lambda part: lax.all_gather(part, axis), x)  67.9 us
    all_gather x2, waiting for transfers between devices, carried_in(): everything = jax.tree.map(lambda part: lax.all_gather(part, axis), x)  52.3 us
    psum x1, waiting for transfers between devices, body(): increment = lax.psum(partial_value, 'mem')  44.9 us
    psum x2, blocking collectives, broadcast(): return lax.psum(jnp.where(mine, x, jnp.zeros_like(x)), axis)  43.5 us
    dot_general x34, matrix products, compose(): jnp.einsum('kjr,jfr->kfr', later[0], earlier[1], precision=highest)  38.5 us
    dynamic_slice x48, local copies, waits for them, and re-layouts, step(): new = combine(before, jax.tree.map(lambda part: part[at], everything))  19.9 us
  transfers between devices with their start and end apart: 3, of which 3 were waited for; matrix products, arithmetic and copies ran while one was open for 2% of the time, Pallas kernels for 0%

commit v1 on v0

v1 whole, which is shorter than its diff:
```python
import functools

import jax
import jax.numpy as jnp
from jax import lax
from jax.experimental import pallas as pl
from jax.experimental.pallas import tpu as pltpu
from jax.sharding import PartitionSpec as P

MESH = pl.DeviceIdType.MESH
F32 = jnp.float32
BF16 = jnp.bfloat16

LON, LAT, MEM = 8, 8, 4
FIELDS, ROWS, COLS = 160, 8, 128
LEVELS, MODES = 32, 8
CHUNK = 16
CHUNKS = FIELDS // CHUNK
STATES = 4 * ROWS


def leak(c):
    series = jnp.ones_like(c)
    for k in range(10, 1, -1):
        series = 1.0 - (c / float(k)) * series
    return c * series


def rising(offset, degree):
    result = jnp.ones_like(offset)
    for k in range(degree):
        result = result * (offset + (k + 1.0)) * (1.0 / (k + 1.0))
    return result


def halves(x):
    high = x.astype(BF16)
    return high, (x - high.astype(F32)).astype(BF16)


def dot3(a, b, dims):
    dot = functools.partial(lax.dot_general, dimension_numbers=(dims, ((), ())), preferred_element_type=F32)
    return dot(a[0], b[0]) + (dot(a[0], b[1]) + dot(a[1], b[0]))


def iota(shape, dim):
    return lax.broadcasted_iota(jnp.int32, shape, dim)


def row_values(shape, lon_decay):
    row = iota(shape, 0)
    c = jnp.zeros(shape, F32)
    for y in range(ROWS):
        c = jnp.where(row // 4 == y, lon_decay[y], c)
    return row, c


def lon_gain(c):
    a = leak(c)
    return a * a * a * jnp.sqrt(a) * 2.5


def kernel(
    direction, residual, members, vert_modes, eig_count, lon_decay, lat_decay, obs_weight,
    hess_out, scal_out,
    dvm, rvm, mvm, ovm, nat, planes, kf_hi, kf_lo, kb_hi, kb_lo, vtab,
    lonc_f, lonc_b, lon_in, fin_f, fin_b, ent_f, ent_b,
    car_f, inc_f, car_b, inc_b, minc, weighted, red_a, red_b, red_c, tile,
    in_sem, out_sem, lon_s, lon_r, lat_s, lat_r, mem_s, mem_r, ra_s, ra_r, rb_s, rb_r, rc_s, rc_r,
):
    me_lon, me_lat, me_mem = lax.axis_index("lon"), lax.axis_index("lat"), lax.axis_index("mem")

    load_d = pltpu.make_async_copy(direction, dvm, in_sem.at[0])
    load_m = pltpu.make_async_copy(members, mvm, in_sem.at[1])
    load_o = pltpu.make_async_copy(obs_weight, ovm, in_sem.at[2])
    load_r = pltpu.make_async_copy(residual, rvm, in_sem.at[3])
    load_d.start()
    load_m.start()
    load_o.start()
    load_r.start()

    barrier = pltpu.get_barrier_semaphore()
    for axis, me, count in (("lon", me_lon, LON), ("lat", me_lat, LAT), ("mem", me_mem, MEM)):
        for delta in range(1, count):
            pl.semaphore_signal(
                barrier, inc=1, device_id={axis: lax.rem(me + delta, count)}, device_id_type=MESH
            )

    row, c_row = row_values((STATES, COLS), lon_decay)
    section = row % 4
    column = iota((STATES, COLS), 1).astype(F32)

    def pick(entries):
        result = entries[3]
        for s in range(3):
            result = jnp.where(section == s, entries[s], result)
        return result

    gain_row = lon_gain(c_row)
    last = COLS - 1.0
    fin_f[...] = pick([rising(last - column, s) for s in range(4)]) * jnp.exp(-(last - column) * c_row)
    fin_b[...] = pick([rising(column, s) for s in range(4)]) * jnp.exp(-column * c_row)
    ent_f[...] = (
        gain_row * pick([rising(column, 3 - s) for s in range(4)]) * jnp.exp(-(column + 1.0) * c_row)
    )
    ent_b[...] = (
        gain_row
        * pick([rising(last - column, 3 - s) for s in range(4)])
        * jnp.exp(-(last - column + 1.0) * c_row)
    )

    source = iota((COLS, COLS), 0)
    target = iota((COLS, COLS), 1)

    def response(offset, y):
        lag = jnp.maximum(offset, 0).astype(F32)
        c = jnp.full((COLS, COLS), lon_decay[y], F32)
        gain = lon_gain(jnp.full((8, COLS), lon_decay[y], F32))[0:1]
        return jnp.where(offset >= 0, rising(lag, 3) * gain * jnp.exp(-lag * c), 0.0)

    def tables_f(y, carry):
        kf_hi[y], kf_lo[y] = halves(response(target - source, y))
        return carry

    def tables_b(y, carry):
        kb_hi[y], kb_lo[y] = halves(response(source - target, y))
        return carry

    lax.fori_loop(0, ROWS, tables_f, 0)

    c_lat = lat_decay[...]
    q = jnp.broadcast_to(jnp.exp(-c_lat), (CHUNK, COLS))
    a_lat = leak(c_lat)
    gain_lat = jnp.broadcast_to(a_lat * a_lat * a_lat * jnp.sqrt(a_lat) * 2.5, (CHUNK, COLS))
    t0 = jnp.broadcast_to(jnp.exp(-8.0 * c_lat), (CHUNK, COLS))

    def lon_states(get_plane, fin, slots):
        total = jnp.zeros((STATES, FIELDS), F32)
        for y in range(ROWS):
            weights = jnp.where(row // 4 == y, fin[...], 0.0)
            total = total + dot3(halves(weights), halves(get_plane(y)), ((1,), (1,)))
        slots[pl.ds((LON - 1) * STATES, STATES), :] = total

    def lon_copy(slots, delta, phase):
        sign = 1 if phase == 0 else LON - 1
        return pltpu.make_async_remote_copy(
            src_ref=slots.at[pl.ds((LON - 1) * STATES, STATES)],
            dst_ref=slots.at[pl.ds((delta - 1) * STATES, STATES)],
            send_sem=lon_s.at[phase, delta - 1],
            recv_sem=lon_r.at[phase, delta - 1],
            device_id={"lon": lax.rem(me_lon + sign * delta, LON)},
            device_id_type=MESH,
        )

    def lon_incoming(slots):
        shape = (STATES, LON * STATES)
        to_row, c = row_values(shape, lon_decay)
        from_col = iota(shape, 1)
        same = (from_col % STATES) // 4 == to_row // 4
        spread = to_row % 4 - from_col % 4
        cells = ((from_col // STATES) * COLS).astype(F32)
        closing = jnp.exp(-cells * c)
        t = [closing * rising(cells - 1.0, k) for k in range(4)]
        circle = jnp.full(shape, float(COLS * LON), F32)
        closed = jnp.exp(-circle * c)
        n = [closed * rising(circle - 1.0, k) for k in range(4)]
        p = [1.0 / (1.0 - n[0])]
        p.append(p[0] * (n[1] * p[0]))
        p.append(p[0] * (n[1] * p[1] + n[2] * p[0]))
        p.append(p[0] * (n[1] * p[2] + n[2] * p[1] + n[3] * p[0]))
        m = [sum(t[j] * p[k - j] for j in range(k + 1)) for k in range(4)]
        mix = jnp.zeros(shape, F32)
        for k in range(4):
            mix = jnp.where(same & (spread == k), m[k], mix)
        incoming = dot3(halves(mix), halves(slots[...]), ((1,), (0,)))
        lon_in[...] = jnp.transpose(incoming)

    def enter(y, ent):
        weights = jnp.where(row // 4 == y, ent[...], 0.0)
        return dot3(halves(lon_in[...]), halves(weights), ((1,), (0,)))

    load_d.wait()

    def d_plane(y):
        return dvm[pl.ds(y, FIELDS, stride=ROWS), :]

    lon_states(d_plane, fin_f, lonc_f)
    pl.semaphore_wait(barrier, LON + LAT + MEM - 3)
    for delta in range(1, LON):
        lon_copy(lonc_f, delta, 0).start()

    def inside_f(y, carry):
        planes[y] = dot3(halves(d_plane(y)), (kf_hi[y], kf_lo[y]), ((1,), (0,)))
        return carry

    lax.fori_loop(0, ROWS, inside_f, 0)

    for delta in range(1, LON):
        lon_copy(lonc_f, delta, 0).wait_recv()
    lon_incoming(lonc_f)

    def entered_f(y):
        planes[y] = planes[y] + enter(y, ent_f)

    for y in range(ROWS):
        entered_f(y)

    def lat_copy(car, inc, c, phase):
        step = 1 if phase == 0 else LAT - 1
        return pltpu.make_async_remote_copy(
            src_ref=car.at[c],
            dst_ref=inc.at[c],
            send_sem=lat_s.at[phase, c],
            recv_sem=lat_r.at[phase, c],
            device_id={"lat": lax.rem(me_lat + step, LAT)},
            device_id_type=MESH,
        )

    def advance(v, f):
        v1 = q * v[0] + f
        v2 = q * v[1] + v1
        v3 = q * v[2] + v2
        v4 = q * v[3] + v3
        return [v1, v2, v3, v4]

    def own_states(get_row, order, car, c):
        v = [jnp.zeros((CHUNK, COLS), F32)] * 4
        for y in order:
            v = advance(v, get_row(y))
        for s in range(4):
            car[c, s] = v[s]

    def pass_on(car, inc, c):
        before = [inc[c, s] for s in range(4)]
        faded = [t0 * b for b in before]
        weight = (1.0, 8.0, 36.0, 120.0)
        for s in range(4):
            total = car[c, s] + faded[s]
            for j in range(s):
                total = total + weight[s - j] * faded[j]
            car[c, s] = total

    first, final = me_lat == 0, me_lat == LAT - 1

    def fields_of(c):
        return pl.ds(pl.multiple_of(c * CHUNK, CHUNK), CHUNK)

    def start_f(c, carry):
        own_states(lambda y: planes[y, fields_of(c), :], range(ROWS), car_f, c)

        @pl.when(first)
        def _():
            lat_copy(car_f, inc_f, c, 0).start()
            inc_f[c] = jnp.zeros((4, CHUNK, COLS), F32)

        return carry

    lax.fori_loop(0, CHUNKS, start_f, 0)

    for e in range(MODES):
        for l in range(LEVELS):
            vtab[l * MODES + e] = jnp.full((8, COLS), vert_modes[e, l], F32)
    lax.fori_loop(0, ROWS, tables_b, 0)
    load_m.wait()
    minc[me_mem] = jnp.zeros((LEVELS * ROWS, COLS), F32)

    lane_mode = iota((8, COLS), 0)

    def active(c):
        return jnp.concatenate(
            [
                jnp.where(lane_mode < eig_count[c * (CHUNK // MODES) + m], 1.0, 0.0)
                for m in range(CHUNK // MODES)
            ]
        )

    group = CHUNK // MODES

    def chain_f(c, carry):
        @pl.when(jnp.logical_not(first))
        def _():
            lat_copy(car_f, inc_f, c, 0).wait_recv()
            pass_on(car_f, inc_f, c)

            @pl.when(jnp.logical_not(final))
            def _():
                lat_copy(car_f, inc_f, c, 0).start()

        v = [inc_f[c, s] for s in range(4)]
        scale = gain_lat * active(c)
        for y in range(ROWS):
            v = advance(v, planes[y, fields_of(c), :])
            nat[pl.ds(c * (CHUNK * ROWS) + y, CHUNK, stride=ROWS), :] = v[3] * scale

        base = pl.multiple_of(c * (CHUNK * ROWS), CHUNK * ROWS)
        w = [nat[pl.ds(base + i * ROWS, ROWS), :] for i in range(CHUNK)]

        def levels(pair, carry):
            ens = [
                mvm[c * group + m, pl.ds(pl.multiple_of(pair * 16, 16), 16), :].astype(F32)
                for m in range(group)
            ]
            for h in range(2):
                total = None
                for m in range(group):
                    profile = None
                    for e in range(MODES):
                        term = vtab[(pair * 2 + h) * MODES + e] * w[m * MODES + e]
                        profile = term if profile is None else profile + term
                    term = ens[m][h * 8 : h * 8 + 8] * profile
                    total = term if total is None else total + term
                at = pl.ds(pl.multiple_of(pair * 16 + h * 8, 8), 8)
                minc[me_mem, at, :] = minc[me_mem, at, :] + total
            return carry

        lax.fori_loop(0, LEVELS // 2, levels, 0)
        return carry

    lax.fori_loop(0, CHUNKS, chain_f, 0)

    def mem_copy(delta):
        return pltpu.make_async_remote_copy(
            src_ref=minc.at[me_mem],
            dst_ref=minc.at[me_mem],
            send_sem=mem_s.at[delta - 1],
            recv_sem=mem_r.at[delta - 1],
            device_id={"mem": lax.rem(me_mem + delta, MEM)},
            device_id_type=MESH,
        )

    for delta in range(1, MEM):
        mem_copy(delta).start()
    load_o.wait()
    for delta in range(1, MEM):
        mem_copy(delta).wait_recv()
    weighted[...] = ovm[...] * ((minc[0] + minc[1]) + (minc[2] + minc[3]))

    def start_b(c, carry):
        def levels(pair, g):
            g = list(g)
            for m in range(group):
                ens = mvm[c * group + m, pl.ds(pl.multiple_of(pair * 16, 16), 16), :].astype(F32)
                both = ens * weighted[pl.ds(pl.multiple_of(pair * 16, 16), 16), :]
                for h in range(2):
                    for e in range(MODES):
                        g[m * MODES + e] = (
                            g[m * MODES + e]
                            + vtab[(pair * 2 + h) * MODES + e] * both[h * 8 : h * 8 + 8]
                        )
            return tuple(g)

        zero = jnp.zeros((8, COLS), F32)
        g = lax.fori_loop(0, LEVELS // 2, levels, (zero,) * CHUNK)
        base = pl.multiple_of(c * (CHUNK * ROWS), CHUNK * ROWS)
        for i in range(CHUNK):
            nat[pl.ds(base + i * ROWS, ROWS), :] = g[i]
        mask = active(c)
        for y in range(ROWS):
            planes[y, fields_of(c), :] = nat[pl.ds(c * (CHUNK * ROWS) + y, CHUNK, stride=ROWS), :] * mask
        own_states(lambda y: planes[y, fields_of(c), :], range(ROWS - 1, -1, -1), car_b, c)

        @pl.when(final)
        def _():
            lat_copy(car_b, inc_b, c, 1).start()
            inc_b[c] = jnp.zeros((4, CHUNK, COLS), F32)

        return carry

    lax.fori_loop(0, CHUNKS, start_b, 0)

    def chain_b(c, carry):
        @pl.when(jnp.logical_not(final))
        def _():
            lat_copy(car_b, inc_b, c, 1).wait_recv()
            pass_on(car_b, inc_b, c)

            @pl.when(jnp.logical_not(first))
            def _():
                lat_copy(car_b, inc_b, c, 1).start()

        v = [inc_b[c, s] for s in range(4)]
        for y in range(ROWS - 1, -1, -1):
            v = advance(v, planes[y, fields_of(c), :])
            planes[y, fields_of(c), :] = v[3] * gain_lat
        return carry

    lax.fori_loop(0, CHUNKS, chain_b, 0)

    lon_states(lambda y: planes[y], fin_b, lonc_b)
    for delta in range(1, LON):
        lon_copy(lonc_b, delta, 1).start()

    def inside_b(y, carry):
        planes[y] = dot3(halves(planes[y]), (kb_hi[y], kb_lo[y]), ((1,), (0,)))
        return carry

    lax.fori_loop(0, ROWS, inside_b, 0)
    load_r.wait()
    for delta in range(1, LON):
        lon_copy(lonc_b, delta, 1).wait_recv()
    lon_incoming(lonc_b)

    sums = [jnp.zeros((8, COLS), F32)] * 4

    def fold(x):
        return jnp.sum(x.reshape(FIELDS // 8, 8, COLS), axis=0)

    for y in range(ROWS):
        at = pl.ds(y, FIELDS, stride=ROWS)
        d, r = dvm[at, :], rvm[at, :]
        h = d + (planes[y] + enter(y, ent_b))
        nat[at, :] = h
        sums = [sums[0] + fold(r * r), sums[1] + fold(d * h), sums[2] + fold(r * h), sums[3] + fold(h * h)]
    store = pltpu.make_async_copy(nat, hess_out, out_sem.at[0])
    store.start()

    for k in range(4):
        tile[pl.ds(k, 1), :] = jnp.sum(sums[k], axis=0, keepdims=True)
    tile[pl.ds(4, 4), :] = jnp.zeros((4, COLS), F32)

    def reduce(axis, me, count, slots, s_sem, r_sem):
        slots[me] = tile[...]

        def copy(delta):
            return pltpu.make_async_remote_copy(
                src_ref=slots.at[me],
                dst_ref=slots.at[me],
                send_sem=s_sem.at[delta - 1],
                recv_sem=r_sem.at[delta - 1],
                device_id={axis: lax.rem(me + delta, count)},
                device_id_type=MESH,
            )

        for delta in range(1, count):
            copy(delta).start()
        for delta in range(1, count):
            copy(delta).wait_recv()
        total = slots[0]
        for k in range(1, count):
            total = total + slots[k]
        tile[...] = total
        return copy

    copy_a = reduce("lon", me_lon, LON, red_a, ra_s, ra_r)
    copy_b = reduce("mem", me_mem, MEM, red_b, rb_s, rb_r)
    copy_c = reduce("lat", me_lat, LAT, red_c, rc_s, rc_r)
    sums = jnp.broadcast_to(jnp.sum(tile[...], axis=1, keepdims=True), (8, COLS))
    rr, dh, rh, hh = (sums[k : k + 1] for k in range(4))
    step = rr / dh
    norm_new = rr - 2.0 * step * rh + step * step * hh
    scal_out[pl.ds(0, 1), :] = step
    scal_out[pl.ds(1, 1), :] = norm_new / rr
    scal_out[pl.ds(2, 6), :] = jnp.zeros((6, COLS), F32)

    store.wait()
    for delta in range(1, LON):
        lon_copy(lonc_f, delta, 0).wait_send()
        lon_copy(lonc_b, delta, 1).wait_send()
        copy_a(delta).wait_send()
    for delta in range(1, MEM):
        mem_copy(delta).wait_send()
        copy_b(delta).wait_send()
    for delta in range(1, LAT):
        copy_c(delta).wait_send()

    @pl.when(jnp.logical_not(final))
    def _():
        def left(c, carry):
            lat_copy(car_f, inc_f, c, 0).wait_send()
            return carry

        lax.fori_loop(0, CHUNKS, left, 0)

    @pl.when(jnp.logical_not(first))
    def _():
        def left(c, carry):
            lat_copy(car_b, inc_b, c, 1).wait_send()
            return carry

        lax.fori_loop(0, CHUNKS, left, 0)


def body(control, residual, direction, members, vert_modes, eig_count, lon_decay, lat_decay, obs_weight):
    rows = FIELDS * ROWS
    any_space = pl.BlockSpec(memory_space=pl.ANY)
    smem = pl.BlockSpec(memory_space=pltpu.SMEM)
    vmem = pl.BlockSpec(memory_space=pltpu.VMEM)
    dma = pltpu.SemaphoreType.DMA
    states = pltpu.VMEM((CHUNKS, 4, CHUNK, COLS), F32)
    table = pltpu.VMEM((ROWS, COLS, COLS), BF16)
    slots = pltpu.VMEM((LON * STATES, FIELDS), F32)
    small = pltpu.VMEM((STATES, COLS), F32)
    hessian, scalars = pl.pallas_call(
        kernel,
        name="cg_step",
        out_shape=(
            jax.ShapeDtypeStruct((rows, COLS), F32),
            jax.ShapeDtypeStruct((8, COLS), F32),
        ),
        in_specs=[any_space, any_space, any_space, smem, smem, smem, vmem, any_space],
        out_specs=(any_space, vmem),
        scratch_shapes=[
            pltpu.VMEM((rows, COLS), F32),
            pltpu.VMEM((rows, COLS), F32),
            pltpu.VMEM((FIELDS // MODES, LEVELS * ROWS, COLS), BF16),
            pltpu.VMEM((LEVELS * ROWS, COLS), F32),
            pltpu.VMEM((rows, COLS), F32),
            pltpu.VMEM((ROWS, FIELDS, COLS), F32),
            table, table, table, table,
            pltpu.VMEM((LEVELS * MODES, 8, COLS), F32),
            slots, slots,
            pltpu.VMEM((FIELDS, STATES), F32),
            small, small, small, small,
            states, states, states, states,
            pltpu.VMEM((MEM, LEVELS * ROWS, COLS), F32),
            pltpu.VMEM((LEVELS * ROWS, COLS), F32),
            pltpu.VMEM((LON, 8, COLS), F32),
            pltpu.VMEM((MEM, 8, COLS), F32),
            pltpu.VMEM((LAT, 8, COLS), F32),
            pltpu.VMEM((8, COLS), F32),
            dma((4,)), dma((1,)),
            dma((2, LON - 1)), dma((2, LON - 1)),
            dma((2, CHUNKS)), dma((2, CHUNKS)),
            dma((MEM - 1,)), dma((MEM - 1,)),
            dma((LON - 1,)), dma((LON - 1,)),
            dma((MEM - 1,)), dma((MEM - 1,)),
            dma((LAT - 1,)), dma((LAT - 1,)),
        ],
        compiler_params=pltpu.CompilerParams(
            collective_id=0, has_side_effects=True, vmem_limit_bytes=60 << 20
        ),
    )(
        direction.reshape(rows, COLS),
        residual.reshape(rows, COLS),
        members.reshape(FIELDS // MODES, LEVELS * ROWS, COLS),
        vert_modes,
        eig_count,
        lon_decay,
        lat_decay.reshape(1, COLS),
        obs_weight.reshape(LEVELS * ROWS, COLS),
    )
    hessian = hessian.reshape(direction.shape)
    step, ratio = scalars[0, 0], scalars[1, 0]
    new_control = control + step * direction
    new_residual = residual - step * hessian
    new_direction = new_residual + ratio * direction
    return new_control, new_residual, new_direction


def solution(mesh):
    field = P("mem", "lat", "lon")
    placed = (
        field, field, field, P("mem", None, "lat", "lon"), P(), P("mem"), P("lat"), P("lon"),
        P(None, "lat", "lon"),
    )
    return jax.shard_map(
        body, mesh=mesh, in_specs=placed, out_specs=(field, field, field), check_vma=False
    )
```

time: 499 us -> 96.4 us (0.19)
  blocking collectives: 261 us -> 0 us
  waiting for transfers between devices: 97.3 us -> 0 us
  Pallas kernels: 0 us -> 89.8 us
  matrix products: 68.8 us -> 0 us
  local copies, waits for them, and re-layouts: 41.7 us -> 1.33 us
  between operations: 17.5 us -> 0.67 us
    psum x4 -> x0, blocking collectives: 194 us -> none  [the longest x1 77.8 us: body(): norm_old = lax.psum(jnp.sum(residual * residual), ('lon', 'lat', 'mem'))]
    pallas_call x0 -> x1, Pallas kernels: none -> 89.8 us  [body(): pl.pallas_call(kernel, name='cg_step', out_shape=(jax.ShapeDtypeStruct((r...]
    dot_general x66 -> x0, matrix products: 68.8 us -> none  [the longest x34 38.5 us: compose(): jnp.einsum('kjr,jfr->kfr', later[0], earlier[1], precision=highest)]
    all_gather x4 -> x0, blocking collectives: 67.9 us -> none  [carried_in(): everything = jax.tree.map(lambda part: lax.all_gather(part, axis), x)]
    all_gather x2 -> x0, waiting for transfers between devices: 52.3 us -> none  [carried_in(): everything = jax.tree.map(lambda part: lax.all_gather(part, axis), x)]
    psum x1 -> x0, waiting for transfers between devices: 44.9 us -> none  [body(): increment = lax.psum(partial_value, 'mem')]
    dynamic_slice x48 -> x0, local copies, waits for them, and re-layouts: 19.9 us -> none  [step(): new = combine(before, jax.tree.map(lambda part: part[at], everything))]
    squeeze x32 -> x0, local copies, waits for them, and re-layouts: 7.44 us -> none  [step(): new = combine(before, jax.tree.map(lambda part: part[at], everything))]
  transfers between devices with their start and end apart: 3 -> 0, of which waited for: 3 -> 0; matrix products, arithmetic and copies ran while one was open for 2% -> 0% of each run, Pallas kernels for 0% -> 0%
where the time goes in v1:
time: 96.4 us; the launch traced here: 95.4 us
  Pallas kernels  89.8 us (93%)
  other arithmetic  3.64 us (4%)
  local copies, waits for them, and re-layouts  1.33 us (1%)
    pallas_call x1, Pallas kernels, body(): pl.pallas_call(kernel, name='cg_step', out_shape=(jax.ShapeDtypeStruct((r...  89.8 us
    add x1, other arithmetic, body(): new_direction = new_residual + ratio * direction  3.64 us

profile of v1, /device:TPU:1, one launch (start us, length us, event | category | flops | bytes accessed | tf_op | source)
XLA Modules:
  0.0 95.4 jit_solution(5282552301825975852)
XLA Ops:
  0.6 0.0 copy-start
  0.6 0.0 copy-start.1
  0.7 0.0 copy-start.2
  0.7 89.8 %cg_step.1 = (f32[1280,128]{1,0:T(8,128)}, f32[8,128]{1,0:T(8,128)}) custom-call(f32[1280,128]{1,0:T(8,128)} %bitcast.10, f32[1280,128]{1,0:T(8,128)} %bitcast.11, bf16[20,256,128]{2,1,0:T(8,128)(2,1)} %bitcast.12, f32[8,32]{1,0:T(8,128)} %vert_modes.1, s32[20]{0:T(128)} %eig_count.1, f32[8]{0:T(128)} %lon_decay.1, f32[1,128]{1,0:T(1,128)} %bitcast.14, ...), custom_call_target="tpu_custom_call" | custom-call | tf_op jit(solution)/shard_map/cg_step/pallas_call | solution.py:493
  90.5 1.3 %fusion = (f32[1,1]{1,0:T(1,128)}, f32[1,1]{1,0:T(1,128)}) fusion(f32[8,128]{1,0:T(8,128)} %get-tuple-element.5), kind=kLoop, calls=%fused_computation.3 | loop fusion | bytes 16 | tf_op jit(solution)/shard_map/slice | solution.py:543
  91.8 0.0 copy-done
  91.8 0.0 copy-done.1
  91.8 0.0 copy-done.2
  91.8 3.6 %multiply_add_fusion = (f32[160,8,128]{2,1,0:T(8,128)}, f32[160,8,128]{2,1,0:T(8,128)}, f32[160,8,128]{2,1,0:T(8,128)}) fusion(f32[160,8,128]{2,1,0:T(8,128)S(1)} %copy-done, f32[]{:T(128)} %bitcast.7, f32[160,8,128]{2,1,0:T(8,128)S(1)} %copy-done.1, f32[1280,128]{1,0:T(8,128)} %get-tuple-element.6, f32[]{:T(128)} %bitcast.5, f32[160,8,128]{2,1,0:T(8,128)S(1)} %copy-done.2), kind=kLoop, calls=%fused_computation.1 | loop fusion | flops 983040 | bytes 4587528 | tf_op jit(solution)/shard_map/add | solution.py:546
Async XLA Ops:
  0.6 91.1 %copy-start = (f32[160,8,128]{2,1,0:T(8,128)S(1)}, f32[160,8,128]{2,1,0:T(8,128)}, u32[]{:S(2)}) copy-start(f32[160,8,128]{2,1,0:T(8,128)} %param.11) | copy-start | bytes 1966084
  0.6 91.1 %copy-start.1 = (f32[160,8,128]{2,1,0:T(8,128)S(1)}, f32[160,8,128]{2,1,0:T(8,128)}, u32[]{:S(2)}) copy-start(f32[160,8,128]{2,1,0:T(8,128)} %param.10) | copy-start | bytes 1966084
  0.7 91.1 %copy-start.2 = (f32[160,8,128]{2,1,0:T(8,128)S(1)}, f32[160,8,128]{2,1,0:T(8,128)}, u32[]{:S(2)}) copy-start(f32[160,8,128]{2,1,0:T(8,128)} %param.9) | copy-start | bytes 1966084

commit v2 on v1

--- a/solution.py
+++ b/solution.py
@@ -14,7 +14,9 @@
 LON, LAT, MEM = 8, 8, 4
 FIELDS, ROWS, COLS = 160, 8, 128
 LEVELS, MODES = 32, 8
-CHUNK = 16
+CHUNK = 8
+GROUP = 2
+LAG = 6
 CHUNKS = FIELDS // CHUNK
 STATES = 4 * ROWS
 
@@ -62,10 +64,10 @@
 
 def kernel(
     direction, residual, members, vert_modes, eig_count, lon_decay, lat_decay, obs_weight,
-    hess_out, scal_out,
+    hess_out, step_out, ratio_out,
     dvm, rvm, mvm, ovm, nat, planes, kf_hi, kf_lo, kb_hi, kb_lo, vtab,
     lonc_f, lonc_b, lon_in, fin_f, fin_b, ent_f, ent_b,
-    car_f, inc_f, car_b, inc_b, minc, weighted, red_a, red_b, red_c, tile,
+    lat_f, lat_b, minc, weighted, red_a, red_b, red_c, tile,
     in_sem, out_sem, lon_s, lon_r, lat_s, lat_r, mem_s, mem_r, ra_s, ra_r, rb_s, rb_r, rc_s, rc_r,
 ):
     me_lon, me_lat, me_mem = lax.axis_index("lon"), lax.axis_index("lat"), lax.axis_index("mem")
@@ -81,7 +83,7 @@
 
     barrier = pltpu.get_barrier_semaphore()
     for axis, me, count in (("lon", me_lon, LON), ("lat", me_lat, LAT), ("mem", me_mem, MEM)):
-        for delta in range(1, count):
+        for delta in (1, LAT - 1) if axis == "lat" else range(1, count):
             pl.semaphore_signal(
                 barrier, inc=1, device_id={axis: lax.rem(me + delta, count)}, device_id_type=MESH
             )
@@ -132,7 +134,6 @@
     q = jnp.broadcast_to(jnp.exp(-c_lat), (CHUNK, COLS))
     a_lat = leak(c_lat)
     gain_lat = jnp.broadcast_to(a_lat * a_lat * a_lat * jnp.sqrt(a_lat) * 2.5, (CHUNK, COLS))
-    t0 = jnp.broadcast_to(jnp.exp(-8.0 * c_lat), (CHUNK, COLS))
 
     def lon_states(get_plane, fin, slots):
         total = jnp.zeros((STATES, FIELDS), F32)
@@ -185,7 +186,7 @@
         return dvm[pl.ds(y, FIELDS, stride=ROWS), :]
 
     lon_states(d_plane, fin_f, lonc_f)
-    pl.semaphore_wait(barrier, LON + LAT + MEM - 3)
+    pl.semaphore_wait(barrier, LON - 1 + 2 + MEM - 1)
     for delta in range(1, LON):
         lon_copy(lonc_f, delta, 0).start()
 
@@ -205,14 +206,17 @@
     for y in range(ROWS):
         entered_f(y)
 
-    def lat_copy(car, inc, c, phase):
-        step = 1 if phase == 0 else LAT - 1
+    OWN, AHEAD_IN, TOTAL_IN, AHEAD_OUT, TOTAL_OUT = range(5)
+
+    def lat_copy(bufs, phase, c, source, ahead, step):
+        sign = step if phase == 0 else -step
+        stream = 0 if ahead else 1
         return pltpu.make_async_remote_copy(
-            src_ref=car.at[c],
-            dst_ref=inc.at[c],
-            send_sem=lat_s.at[phase, c],
-            recv_sem=lat_r.at[phase, c],
-            device_id={"lat": lax.rem(me_lat + step, LAT)},
+            src_ref=bufs.at[source, c],
+            dst_ref=bufs.at[AHEAD_IN if ahead else TOTAL_IN, c],
+            send_sem=lat_s.at[phase, stream, c],
+            recv_sem=lat_r.at[phase, stream, c],
+            device_id={"lat": lax.rem(me_lat + (LAT + sign), LAT)},
             device_id_type=MESH,
         )
 
@@ -223,36 +227,119 @@
         v4 = q * v[3] + v3
         return [v1, v2, v3, v4]
 
-    def own_states(get_row, order, car, c):
+    def own_states(get_row, order, bufs, c):
         v = [jnp.zeros((CHUNK, COLS), F32)] * 4
         for y in order:
             v = advance(v, get_row(y))
         for s in range(4):
-            car[c, s] = v[s]
-
-    def pass_on(car, inc, c):
-        before = [inc[c, s] for s in range(4)]
-        faded = [t0 * b for b in before]
-        weight = (1.0, 8.0, 36.0, 120.0)
+            bufs[OWN, c, s] = v[s]
+
+    def transition(cells):
+        closing = jnp.exp(-cells * c_lat)
+        offset = jnp.zeros((1, COLS), F32) + (cells - 1.0)
+        return [jnp.broadcast_to(closing * rising(offset, k), (CHUNK, COLS)) for k in range(4)]
+
+    one_block = transition(float(ROWS))
+
+    def add_moved(move, moved, fixed, result, bufs, c):
+        v = [bufs[moved, c, s] for s in range(4)]
+        w = [bufs[fixed, c, s] for s in range(4)]
         for s in range(4):
-            total = car[c, s] + faded[s]
-            for j in range(s):
-                total = total + weight[s - j] * faded[j]
-            car[c, s] = total
-
-    first, final = me_lat == 0, me_lat == LAT - 1
+            total = w[s]
+            for j in range(s + 1):
+                total = total + move[s - j] * v[j]
+            bufs[result, c, s] = total
+
+    def is_in(p, *places):
+        return functools.reduce(jnp.logical_or, [p == k for k in places])
+
+    def places_of(phase):
+        p = me_lat if phase == 0 else LAT - 1 - me_lat
+        blocks = jnp.where(p < 4, 3 - p, p - 4)
+        return p, transition((blocks * ROWS).astype(F32))
+
+    def lat_begin(bufs, phase, p, c):
+        @pl.when(is_in(p, 0, 4))
+        def _():
+            lat_copy(bufs, phase, c, OWN, True, 1).start()
+
+        @pl.when(p == 3)
+        def _():
+            lat_copy(bufs, phase, c, OWN, False, -1).start()
+
+        @pl.when(p == 0)
+        def _():
+            bufs[AHEAD_IN, c] = jnp.zeros((4, CHUNK, COLS), F32)
+
+    def lat_streams(bufs, phase, p, far):
+        late_ahead = jnp.where(p == 2, LAG, 0)
+        late_total = jnp.where(p == 1, LAG, 0)
+
+        def step(t, carry):
+            a, b = t - late_ahead, t - late_total
+
+            @pl.when(is_in(p, 1, 2, 3, 5, 6) & (a >= 0) & (a < CHUNKS))
+            def _():
+                lat_copy(bufs, phase, a, AHEAD_OUT, True, 1).wait_recv()
+                add_moved(one_block, AHEAD_IN, OWN, AHEAD_OUT, bufs, a)
+                lat_copy(bufs, phase, a, AHEAD_OUT, True, 1).start()
+
+            @pl.when((p < 3) & (b >= 0) & (b < CHUNKS))
+            def _():
+                lat_copy(bufs, phase, b, TOTAL_OUT, False, -1).wait_recv()
+                add_moved(far, OWN, TOTAL_IN, TOTAL_OUT, bufs, b)
+                lat_copy(bufs, phase, b, TOTAL_OUT, False, -1).start()
+
+            return carry
+
+        lax.fori_loop(0, CHUNKS + LAG, step, 0)
+
+    def lat_finish(bufs, phase, p, far, c):
+        @pl.when(is_in(p, 4, 7))
+        def _():
+            lat_copy(bufs, phase, c, AHEAD_OUT, True, 1).wait_recv()
+
+        @pl.when(p == 4)
+        def _():
+            lat_copy(bufs, phase, c, AHEAD_IN, False, 1).start()
+
+        @pl.when(p > 4)
+        def _():
+            lat_copy(bufs, phase, c, TOTAL_OUT, False, -1).wait_recv()
+
+        @pl.when(p == 7)
+        def _():
+            lat_copy(bufs, phase, c, TOTAL_IN, False, -1).start()
+
+        @pl.when(p > 4)
+        def _():
+            add_moved(far, TOTAL_IN, AHEAD_IN, AHEAD_IN, bufs, c)
+
+        return [bufs[AHEAD_IN, c, s] for s in range(4)]
+
+    def lat_left(bufs, phase, p):
+        def left(c, carry):
+            @pl.when(p < 7)
+            def _():
+                lat_copy(bufs, phase, c, AHEAD_OUT, True, 1).wait_send()
+
+            @pl.when((p < 5) | (p == 7))
+            def _():
+                lat_copy(bufs, phase, c, TOTAL_OUT, False, -1).wait_send()
+
+            return carry
+
+        lax.fori_loop(0, CHUNKS, left, 0)
+
+    p_f, far_f = places_of(0)
+    p_b, far_b = places_of(1)
 
     def fields_of(c):
         return pl.ds(pl.multiple_of(c * CHUNK, CHUNK), CHUNK)
 
     def start_f(c, carry):
-        own_states(lambda y: planes[y, fields_of(c), :], range(ROWS), car_f, c)
-
-        @pl.when(first)
-        def _():
-            lat_copy(car_f, inc_f, c, 0).start()
-            inc_f[c] = jnp.zeros((4, CHUNK, COLS), F32)
-
+        own_states(lambda y: planes[y, fields_of(c), :], range(ROWS), lat_f, c)
+        lat_begin(lat_f, 0, p_f, c)
         return carry
 
     lax.fori_loop(0, CHUNKS, start_f, 0)
@@ -264,48 +351,34 @@
     load_m.wait()
     minc[me_mem] = jnp.zeros((LEVELS * ROWS, COLS), F32)
 
-    lane_mode = iota((8, COLS), 0)
+    mode = iota((CHUNK, COLS), 0)
 
     def active(c):
-        return jnp.concatenate(
-            [
-                jnp.where(lane_mode < eig_count[c * (CHUNK // MODES) + m], 1.0, 0.0)
-                for m in range(CHUNK // MODES)
-            ]
-        )
-
-    group = CHUNK // MODES
-
-    def chain_f(c, carry):
-        @pl.when(jnp.logical_not(first))
-        def _():
-            lat_copy(car_f, inc_f, c, 0).wait_recv()
-            pass_on(car_f, inc_f, c)
-
-            @pl.when(jnp.logical_not(final))
-            def _():
-                lat_copy(car_f, inc_f, c, 0).start()
-
-        v = [inc_f[c, s] for s in range(4)]
-        scale = gain_lat * active(c)
-        for y in range(ROWS):
-            v = advance(v, planes[y, fields_of(c), :])
-            nat[pl.ds(c * (CHUNK * ROWS) + y, CHUNK, stride=ROWS), :] = v[3] * scale
-
-        base = pl.multiple_of(c * (CHUNK * ROWS), CHUNK * ROWS)
-        w = [nat[pl.ds(base + i * ROWS, ROWS), :] for i in range(CHUNK)]
+        return jnp.where(mode < eig_count[c], 1.0, 0.0)
+
+    lat_streams(lat_f, 0, p_f, far_f)
+
+    def chain_f(g, carry):
+        w = []
+        for k in range(GROUP):
+            c = g * GROUP + k
+            v = lat_finish(lat_f, 0, p_f, far_f, c)
+            scale = gain_lat * active(c)
+            for y in range(ROWS):
+                v = advance(v, planes[y, fields_of(c), :])
+                nat[pl.ds(c * (CHUNK * ROWS) + y, CHUNK, stride=ROWS), :] = v[3] * scale
+            base = pl.multiple_of(c * (CHUNK * ROWS), CHUNK * ROWS)
+            w.append([nat[pl.ds(base + e * ROWS, ROWS), :] for e in range(MODES)])
 
         def levels(pair, carry):
-            ens = [
-                mvm[c * group + m, pl.ds(pl.multiple_of(pair * 16, 16), 16), :].astype(F32)
-                for m in range(group)
-            ]
+            at = pl.ds(pl.multiple_of(pair * 16, 16), 16)
+            ens = [mvm[g * GROUP + m, at, :].astype(F32) for m in range(GROUP)]
             for h in range(2):
                 total = None
-                for m in range(group):
+                for m in range(GROUP):
                     profile = None
                     for e in range(MODES):
-                        term = vtab[(pair * 2 + h) * MODES + e] * w[m * MODES + e]
+                        term = vtab[(pair * 2 + h) * MODES + e] * w[m][e]
                         profile = term if profile is None else profile + term
                     term = ens[m][h * 8 : h * 8 + 8] * profile
                     total = term if total is None else total + term
@@ -316,7 +389,7 @@
         lax.fori_loop(0, LEVELS // 2, levels, 0)
         return carry
 
-    lax.fori_loop(0, CHUNKS, chain_f, 0)
+    lax.fori_loop(0, CHUNKS // GROUP, chain_f, 0)
 
     def mem_copy(delta):
         return pltpu.make_async_remote_copy(
@@ -335,50 +408,42 @@
         mem_copy(delta).wait_recv()
     weighted[...] = ovm[...] * ((minc[0] + minc[1]) + (minc[2] + minc[3]))
 
-    def start_b(c, carry):
-        def levels(pair, g):
-            g = list(g)
-            for m in range(group):
-                ens = mvm[c * group + m, pl.ds(pl.multiple_of(pair * 16, 16), 16), :].astype(F32)
-                both = ens * weighted[pl.ds(pl.multiple_of(pair * 16, 16), 16), :]
+    def start_b(g, carry):
+        def levels(pair, total):
+            total = list(total)
+            at = pl.ds(pl.multiple_of(pair * 16, 16), 16)
+            weight = weighted[at, :]
+            for m in range(GROUP):
+                both = mvm[g * GROUP + m, at, :].astype(F32) * weight
                 for h in range(2):
                     for e in range(MODES):
-                        g[m * MODES + e] = (
-                            g[m * MODES + e]
+                        total[m * MODES + e] = (
+                            total[m * MODES + e]
                             + vtab[(pair * 2 + h) * MODES + e] * both[h * 8 : h * 8 + 8]
                         )
-            return tuple(g)
+            return tuple(total)
 
         zero = jnp.zeros((8, COLS), F32)
-        g = lax.fori_loop(0, LEVELS // 2, levels, (zero,) * CHUNK)
-        base = pl.multiple_of(c * (CHUNK * ROWS), CHUNK * ROWS)
-        for i in range(CHUNK):
-            nat[pl.ds(base + i * ROWS, ROWS), :] = g[i]
-        mask = active(c)
-        for y in range(ROWS):
-            planes[y, fields_of(c), :] = nat[pl.ds(c * (CHUNK * ROWS) + y, CHUNK, stride=ROWS), :] * mask
-        own_states(lambda y: planes[y, fields_of(c), :], range(ROWS - 1, -1, -1), car_b, c)
-
-        @pl.when(final)
-        def _():
-            lat_copy(car_b, inc_b, c, 1).start()
-            inc_b[c] = jnp.zeros((4, CHUNK, COLS), F32)
-
-        return carry
-
-    lax.fori_loop(0, CHUNKS, start_b, 0)
+        total = lax.fori_loop(0, LEVELS // 2, levels, (zero,) * (GROUP * MODES))
+        for k in range(GROUP):
+            c = g * GROUP + k
+            base = pl.multiple_of(c * (CHUNK * ROWS), CHUNK * ROWS)
+            for e in range(MODES):
+                nat[pl.ds(base + e * ROWS, ROWS), :] = total[k * MODES + e]
+            mask = active(c)
+            for y in range(ROWS):
+                planes[y, fields_of(c), :] = (
+                    nat[pl.ds(c * (CHUNK * ROWS) + y, CHUNK, stride=ROWS), :] * mask
+                )
+            own_states(lambda y: planes[y, fields_of(c), :], range(ROWS - 1, -1, -1), lat_b, c)
+            lat_begin(lat_b, 1, p_b, c)
+        return carry
+
+    lax.fori_loop(0, CHUNKS // GROUP, start_b, 0)
+    lat_streams(lat_b, 1, p_b, far_b)
 
     def chain_b(c, carry):
-        @pl.when(jnp.logical_not(final))
-        def _():
-            lat_copy(car_b, inc_b, c, 1).wait_recv()
-            pass_on(car_b, inc_b, c)
-
-            @pl.when(jnp.logical_not(first))
-            def _():
-                lat_copy(car_b, inc_b, c, 1).start()
-
-        v = [inc_b[c, s] for s in range(4)]
+        v = lat_finish(lat_b, 1, p_b, far_b, c)
         for y in range(ROWS - 1, -1, -1):
             v = advance(v, planes[y, fields_of(c), :])
             planes[y, fields_of(c), :] = v[3] * gain_lat
@@ -448,9 +513,8 @@
     rr, dh, rh, hh = (sums[k : k + 1] for k in range(4))
     step = rr / dh
     norm_new = rr - 2.0 * step * rh + step * step * hh
-    scal_out[pl.ds(0, 1), :] = step
-    scal_out[pl.ds(1, 1), :] = norm_new / rr
-    scal_out[pl.ds(2, 6), :] = jnp.zeros((6, COLS), F32)
+    step_out[0, 0] = step[0, 0]
+    ratio_out[0, 0] = (norm_new / rr)[0, 0]
 
     store.wait()
     for delta in range(1, LON):
@@ -463,21 +527,8 @@
     for delta in range(1, LAT):
         copy_c(delta).wait_send()
 
-    @pl.when(jnp.logical_not(final))
-    def _():
-        def left(c, carry):
-            lat_copy(car_f, inc_f, c, 0).wait_send()
-            return carry
-
-        lax.fori_loop(0, CHUNKS, left, 0)
-
-    @pl.when(jnp.logical_not(first))
-    def _():
-        def left(c, carry):
-            lat_copy(car_b, inc_b, c, 1).wait_send()
-            return carry
-
-        lax.fori_loop(0, CHUNKS, left, 0)
+    lat_left(lat_f, 0, p_f)
+    lat_left(lat_b, 1, p_b)
 
 
 def body(control, residual, direction, members, vert_modes, eig_count, lon_decay, lat_decay, obs_weight):
@@ -486,19 +537,20 @@
     smem = pl.BlockSpec(memory_space=pltpu.SMEM)
     vmem = pl.BlockSpec(memory_space=pltpu.VMEM)
     dma = pltpu.SemaphoreType.DMA
-    states = pltpu.VMEM((CHUNKS, 4, CHUNK, COLS), F32)
+    states = pltpu.VMEM((5, CHUNKS, 4, CHUNK, COLS), F32)
     table = pltpu.VMEM((ROWS, COLS, COLS), BF16)
     slots = pltpu.VMEM((LON * STATES, FIELDS), F32)
     small = pltpu.VMEM((STATES, COLS), F32)
-    hessian, scalars = pl.pallas_call(
+    one = jax.ShapeDtypeStruct((1, 1), F32)
+    hessian, step, ratio = pl.pallas_call(
         kernel,
         name="cg_step",
         out_shape=(
             jax.ShapeDtypeStruct((rows, COLS), F32),
-            jax.ShapeDtypeStruct((8, COLS), F32),
+            one, one,
         ),
         in_specs=[any_space, any_space, any_space, smem, smem, smem, vmem, any_space],
-        out_specs=(any_space, vmem),
+        out_specs=(any_space, smem, smem),
         scratch_shapes=[
             pltpu.VMEM((rows, COLS), F32),
             pltpu.VMEM((rows, COLS), F32),
@@ -511,7 +563,7 @@
             slots, slots,
             pltpu.VMEM((FIELDS, STATES), F32),
             small, small, small, small,
-            states, states, states, states,
+            states, states,
             pltpu.VMEM((MEM, LEVELS * ROWS, COLS), F32),
             pltpu.VMEM((LEVELS * ROWS, COLS), F32),
             pltpu.VMEM((LON, 8, COLS), F32),
@@ -520,7 +572,7 @@
             pltpu.VMEM((8, COLS), F32),
             dma((4,)), dma((1,)),
             dma((2, LON - 1)), dma((2, LON - 1)),
-            dma((2, CHUNKS)), dma((2, CHUNKS)),
+            dma((2, 2, CHUNKS)), dma((2, 2, CHUNKS)),
             dma((MEM - 1,)), dma((MEM - 1,)),
             dma((LON - 1,)), dma((LON - 1,)),
             dma((MEM - 1,)), dma((MEM - 1,)),
@@ -540,7 +592,7 @@
         obs_weight.reshape(LEVELS * ROWS, COLS),
     )
     hessian = hessian.reshape(direction.shape)
-    step, ratio = scalars[0, 0], scalars[1, 0]
+    step, ratio = step.reshape(()), ratio.reshape(())
     new_control = control + step * direction
     new_residual = residual - step * hessian
     new_direction = new_residual + ratio * direction

time: 96.4 us -> 90.7 us (0.941)
  Pallas kernels: 89.8 us -> 86.1 us
  local copies, waits for them, and re-layouts: 1.33 us -> 0.01 us
    pallas_call x1, Pallas kernels: 89.8 us -> 86.1 us  [body(): pl.pallas_call(kernel, name='cg_step', out_shape=(jax.ShapeDtypeStruct((r...]
    slice x1 -> x0, local copies, waits for them, and re-layouts: 1.32 us -> none  [body(): step, ratio = (scalars[0, 0], scalars[1, 0])]
where the time goes in v2:
time: 90.7 us; the launch traced here: 90.6 us
  Pallas kernels  86.1 us (95%)
  other arithmetic  3.75 us (4%)
    pallas_call x1, Pallas kernels, body(): pl.pallas_call(kernel, name='cg_step', out_shape=(jax.ShapeDtypeStruct((r...  86.1 us
    add x1, other arithmetic, body(): new_direction = new_residual + ratio * direction  3.75 us

profile of v2, /device:TPU:1, one launch (start us, length us, event | category | flops | bytes accessed | tf_op | source)
XLA Modules:
  0.0 90.6 jit_solution(14473708401558514396)
XLA Ops:
  0.6 0.0 copy-start
  0.6 0.0 copy-start.1
  0.7 0.0 copy-start.2
  0.7 86.1 %cg_step.1 = (f32[1280,128]{1,0:T(8,128)}, f32[1,1]{1,0:T(1,128)}, f32[1,1]{1,0:T(1,128)}) custom-call(f32[1280,128]{1,0:T(8,128)} %bitcast.10, f32[1280,128]{1,0:T(8,128)} %bitcast.11, bf16[20,256,128]{2,1,0:T(8,128)(2,1)} %bitcast.12, f32[8,32]{1,0:T(8,128)} %vert_modes.1, s32[20]{0:T(128)} %eig_count.1, f32[8]{0:T(128)} %lon_decay.1, f32[1,128]{1,0:T(1,128)} %bitcast.14, ...), custom_call_target="tpu_custom_call" | custom-call | tf_op jit(solution)/shard_map/cg_step/pallas_call | solution.py:545
  86.8 0.0 copy-done
  86.8 0.0 copy-done.1
  86.8 0.0 copy-done.2
  86.8 3.8 %multiply_add_fusion = (f32[160,8,128]{2,1,0:T(8,128)}, f32[160,8,128]{2,1,0:T(8,128)}, f32[160,8,128]{2,1,0:T(8,128)}) fusion(f32[160,8,128]{2,1,0:T(8,128)S(1)} %copy-done, f32[]{:T(128)} %bitcast.7, f32[160,8,128]{2,1,0:T(8,128)S(1)} %copy-done.1, f32[1280,128]{1,0:T(8,128)} %get-tuple-element.7, f32[]{:T(128)} %bitcast.5, f32[160,8,128]{2,1,0:T(8,128)S(1)} %copy-done.2), kind=kLoop, calls=%fused_computation.1 | loop fusion | flops 983040 | bytes 4587528 | tf_op jit(solution)/shard_map/add | solution.py:598
Async XLA Ops:
  0.6 86.1 %copy-start = (f32[160,8,128]{2,1,0:T(8,128)S(1)}, f32[160,8,128]{2,1,0:T(8,128)}, u32[]{:S(2)}) copy-start(f32[160,8,128]{2,1,0:T(8,128)} %param.11) | copy-start | bytes 1966084
  0.6 86.1 %copy-start.1 = (f32[160,8,128]{2,1,0:T(8,128)S(1)}, f32[160,8,128]{2,1,0:T(8,128)}, u32[]{:S(2)}) copy-start(f32[160,8,128]{2,1,0:T(8,128)} %param.10) | copy-start | bytes 1966084
  0.7 86.1 %copy-start.2 = (f32[160,8,128]{2,1,0:T(8,128)S(1)}, f32[160,8,128]{2,1,0:T(8,128)}, u32[]{:S(2)}) copy-start(f32[160,8,128]{2,1,0:T(8,128)} %param.9) | copy-start | bytes 1966084

commit v3 on v2

--- a/solution.py
+++ b/solution.py
@@ -16,8 +16,10 @@
 LEVELS, MODES = 32, 8
 CHUNK = 8
 GROUP = 2
-LAG = 6
+LAG = 12
 CHUNKS = FIELDS // CHUNK
+GROUPS = ((128, 32), (0, 128))
+FIRST = 16
 STATES = 4 * ROWS
 
 
@@ -63,23 +65,14 @@
 
 
 def kernel(
-    direction, residual, members, vert_modes, eig_count, lon_decay, lat_decay, obs_weight,
+    direction, residual, members, vert_modes_in, eig_count_in, lon_decay_in, lat_decay_in, obs_weight,
     hess_out, step_out, ratio_out,
-    dvm, rvm, mvm, ovm, nat, planes, kf_hi, kf_lo, kb_hi, kb_lo, vtab,
-    lonc_f, lonc_b, lon_in, fin_f, fin_b, ent_f, ent_b,
-    lat_f, lat_b, minc, weighted, red_a, red_b, red_c, tile,
-    in_sem, out_sem, lon_s, lon_r, lat_s, lat_r, mem_s, mem_r, ra_s, ra_r, rb_s, rb_r, rc_s, rc_r,
+    vert_modes, eig_count, lon_decay, lat_decay, dvm, rvm, mvm, ovm, nat, planes, kf_hi, kf_lo, kb_hi, kb_lo, vtab,
+    lon_fa, lon_fb, lon_ba, lon_bb, in_a, in_b, mix_hi, mix_lo, fin_f, fin_b, ent_f, ent_b,
+    lat_f, lat_b, minc, weighted, red_a, red_c, tile,
+    in_sem, out_sem, lon_s, lon_r, lat_s, lat_r, mem_s, mem_r, ra_s, ra_r, rc_s, rc_r,
 ):
     me_lon, me_lat, me_mem = lax.axis_index("lon"), lax.axis_index("lat"), lax.axis_index("mem")
-
-    load_d = pltpu.make_async_copy(direction, dvm, in_sem.at[0])
-    load_m = pltpu.make_async_copy(members, mvm, in_sem.at[1])
-    load_o = pltpu.make_async_copy(obs_weight, ovm, in_sem.at[2])
-    load_r = pltpu.make_async_copy(residual, rvm, in_sem.at[3])
-    load_d.start()
-    load_m.start()
-    load_o.start()
-    load_r.start()
 
     barrier = pltpu.get_barrier_semaphore()
     for axis, me, count in (("lon", me_lon, LON), ("lat", me_lat, LAT), ("mem", me_mem, MEM)):
@@ -87,6 +80,21 @@
             pl.semaphore_signal(
                 barrier, inc=1, device_id={axis: lax.rem(me + delta, count)}, device_id_type=MESH
             )
+
+    load_d = pltpu.make_async_copy(direction, dvm, in_sem.at[0])
+    load_m = pltpu.make_async_copy(members, mvm, in_sem.at[1])
+    load_o = pltpu.make_async_copy(obs_weight, ovm, in_sem.at[2])
+    load_r = pltpu.make_async_copy(residual, rvm, in_sem.at[3])
+    small = [
+        pltpu.make_async_copy(lon_decay_in, lon_decay, in_sem.at[4]),
+        pltpu.make_async_copy(lat_decay_in, lat_decay, in_sem.at[5]),
+        pltpu.make_async_copy(vert_modes_in, vert_modes, in_sem.at[6]),
+        pltpu.make_async_copy(eig_count_in, eig_count, in_sem.at[7]),
+    ]
+    for load in (*small, load_d, load_m, load_o, load_r):
+        load.start()
+    for load in small:
+        load.wait()
 
     row, c_row = row_values((STATES, COLS), lon_decay)
     section = row % 4
@@ -135,25 +143,30 @@
     a_lat = leak(c_lat)
     gain_lat = jnp.broadcast_to(a_lat * a_lat * a_lat * jnp.sqrt(a_lat) * 2.5, (CHUNK, COLS))
 
-    def lon_states(get_plane, fin, slots):
-        total = jnp.zeros((STATES, FIELDS), F32)
+    lon_slots = ((lon_fa, lon_fb), (lon_ba, lon_bb))
+    lon_in = (in_a, in_b)
+
+    def lon_states(get_plane, fin, phase, g):
+        first, count = GROUPS[g]
+        total = jnp.zeros((STATES, count), F32)
         for y in range(ROWS):
             weights = jnp.where(row // 4 == y, fin[...], 0.0)
-            total = total + dot3(halves(weights), halves(get_plane(y)), ((1,), (1,)))
-        slots[pl.ds((LON - 1) * STATES, STATES), :] = total
-
-    def lon_copy(slots, delta, phase):
+            total = total + dot3(halves(weights), halves(get_plane(y, first, count)), ((1,), (1,)))
+        lon_slots[phase][g][pl.ds((LON - 1) * STATES, STATES), :] = total
+
+    def lon_copy(phase, g, delta):
         sign = 1 if phase == 0 else LON - 1
+        slots = lon_slots[phase][g]
         return pltpu.make_async_remote_copy(
             src_ref=slots.at[pl.ds((LON - 1) * STATES, STATES)],
             dst_ref=slots.at[pl.ds((delta - 1) * STATES, STATES)],
-            send_sem=lon_s.at[phase, delta - 1],
-            recv_sem=lon_r.at[phase, delta - 1],
+            send_sem=lon_s.at[phase, g, delta - 1],
+            recv_sem=lon_r.at[phase, g, delta - 1],
             device_id={"lon": lax.rem(me_lon + sign * delta, LON)},
             device_id_type=MESH,
         )
 
-    def lon_incoming(slots):
+    def lon_mix():
         shape = (STATES, LON * STATES)
         to_row, c = row_values(shape, lon_decay)
         from_col = iota(shape, 1)
@@ -173,22 +186,31 @@
         mix = jnp.zeros(shape, F32)
         for k in range(4):
             mix = jnp.where(same & (spread == k), m[k], mix)
-        incoming = dot3(halves(mix), halves(slots[...]), ((1,), (0,)))
-        lon_in[...] = jnp.transpose(incoming)
-
-    def enter(y, ent):
+        mix_hi[...], mix_lo[...] = halves(mix)
+
+    def lon_incoming(phase, g):
+        for delta in range(1, LON):
+            lon_copy(phase, g, delta).wait_recv()
+        mix = (mix_hi[...], mix_lo[...])
+        incoming = dot3(mix, halves(lon_slots[phase][g][...]), ((1,), (0,)))
+        lon_in[g][...] = jnp.transpose(incoming)
+
+    def enter(y, ent, g):
         weights = jnp.where(row // 4 == y, ent[...], 0.0)
-        return dot3(halves(lon_in[...]), halves(weights), ((1,), (0,)))
-
+        return dot3(halves(lon_in[g][...]), halves(weights), ((1,), (0,)))
+
+    lon_mix()
     load_d.wait()
 
-    def d_plane(y):
-        return dvm[pl.ds(y, FIELDS, stride=ROWS), :]
-
-    lon_states(d_plane, fin_f, lonc_f)
+    def d_plane(y, first=0, count=FIELDS):
+        return dvm[pl.ds(first * ROWS + y, count, stride=ROWS), :]
+
+    lon_states(d_plane, fin_f, 0, 0)
+    lon_states(d_plane, fin_f, 0, 1)
     pl.semaphore_wait(barrier, LON - 1 + 2 + MEM - 1)
-    for delta in range(1, LON):
-        lon_copy(lonc_f, delta, 0).start()
+    for g in range(2):
+        for delta in range(1, LON):
+            lon_copy(0, g, delta).start()
 
     def inside_f(y, carry):
         planes[y] = dot3(halves(d_plane(y)), (kf_hi[y], kf_lo[y]), ((1,), (0,)))
@@ -196,15 +218,11 @@
 
     lax.fori_loop(0, ROWS, inside_f, 0)
 
-    for delta in range(1, LON):
-        lon_copy(lonc_f, delta, 0).wait_recv()
-    lon_incoming(lonc_f)
-
-    def entered_f(y):
-        planes[y] = planes[y] + enter(y, ent_f)
-
-    for y in range(ROWS):
-        entered_f(y)
+    def entered_f(g):
+        lon_incoming(0, g)
+        at = pl.ds(*GROUPS[g])
+        for y in range(ROWS):
+            planes[y, at, :] = planes[y, at, :] + enter(y, ent_f, g)
 
     OWN, AHEAD_IN, TOTAL_IN, AHEAD_OUT, TOTAL_OUT = range(5)
 
@@ -271,20 +289,31 @@
         def _():
             bufs[AHEAD_IN, c] = jnp.zeros((4, CHUNK, COLS), F32)
 
-    def lat_streams(bufs, phase, p, far):
-        late_ahead = jnp.where(p == 2, LAG, 0)
-        late_total = jnp.where(p == 1, LAG, 0)
+    def lat_streams(bufs, phase, p, far, prepare=None):
+        wait_all = 0 if prepare is None else CHUNKS
+        late_ahead = jnp.where(p == 2, LAG, jnp.where(p == 3, wait_all, 0))
+        late_total = jnp.where(p == 1, LAG, jnp.where(p == 0, wait_all, 0))
+
+        def chunk_of(t):
+            return lax.rem(t + (FIRST if phase == 0 else 0) + CHUNKS, CHUNKS)
 
         def step(t, carry):
-            a, b = t - late_ahead, t - late_total
-
-            @pl.when(is_in(p, 1, 2, 3, 5, 6) & (a >= 0) & (a < CHUNKS))
+            a_at, b_at = t - late_ahead, t - late_total
+            a, b = chunk_of(a_at), chunk_of(b_at)
+            if prepare is not None:
+
+                @pl.when((lax.rem(t, GROUP) == 0) & (t < CHUNKS))
+                def _():
+                    prepare(t // GROUP)
+
+
+            @pl.when(is_in(p, 1, 2, 3, 5, 6) & (a_at >= 0) & (a_at < CHUNKS))
             def _():
                 lat_copy(bufs, phase, a, AHEAD_OUT, True, 1).wait_recv()
                 add_moved(one_block, AHEAD_IN, OWN, AHEAD_OUT, bufs, a)
                 lat_copy(bufs, phase, a, AHEAD_OUT, True, 1).start()
 
-            @pl.when((p < 3) & (b >= 0) & (b < CHUNKS))
+            @pl.when((p < 3) & (b_at >= 0) & (b_at < CHUNKS))
             def _():
                 lat_copy(bufs, phase, b, TOTAL_OUT, False, -1).wait_recv()
                 add_moved(far, OWN, TOTAL_IN, TOTAL_OUT, bufs, b)
@@ -292,7 +321,7 @@
 
             return carry
 
-        lax.fori_loop(0, CHUNKS + LAG, step, 0)
+        lax.fori_loop(0, CHUNKS + max(LAG, wait_all), step, 0)
 
     def lat_finish(bufs, phase, p, far, c):
         @pl.when(is_in(p, 4, 7))
@@ -342,7 +371,10 @@
         lat_begin(lat_f, 0, p_f, c)
         return carry
 
-    lax.fori_loop(0, CHUNKS, start_f, 0)
+    entered_f(0)
+    lax.fori_loop(FIRST, CHUNKS, start_f, 0)
+    entered_f(1)
+    lax.fori_loop(0, FIRST, start_f, 0)
 
     for e in range(MODES):
         for l in range(LEVELS):
@@ -358,7 +390,8 @@
 
     lat_streams(lat_f, 0, p_f, far_f)
 
-    def chain_f(g, carry):
+    def chain_f(turn, carry):
+        g = lax.rem(turn + FIRST // GROUP, CHUNKS // GROUP)
         w = []
         for k in range(GROUP):
             c = g * GROUP + k
@@ -408,7 +441,7 @@
         mem_copy(delta).wait_recv()
     weighted[...] = ovm[...] * ((minc[0] + minc[1]) + (minc[2] + minc[3]))
 
-    def start_b(g, carry):
+    def start_b(g):
         def levels(pair, total):
             total = list(total)
             at = pl.ds(pl.multiple_of(pair * 16, 16), 16)
@@ -437,10 +470,8 @@
                 )
             own_states(lambda y: planes[y, fields_of(c), :], range(ROWS - 1, -1, -1), lat_b, c)
             lat_begin(lat_b, 1, p_b, c)
-        return carry
-
-    lax.fori_loop(0, CHUNKS // GROUP, start_b, 0)
-    lat_streams(lat_b, 1, p_b, far_b)
+
+    lat_streams(lat_b, 1, p_b, far_b, start_b)
 
     def chain_b(c, carry):
         v = lat_finish(lat_b, 1, p_b, far_b, c)
@@ -449,11 +480,17 @@
             planes[y, fields_of(c), :] = v[3] * gain_lat
         return carry
 
-    lax.fori_loop(0, CHUNKS, chain_b, 0)
-
-    lon_states(lambda y: planes[y], fin_b, lonc_b)
+    def z_plane(y, first, count):
+        return planes[y, pl.ds(first, count), :]
+
+    lax.fori_loop(0, FIRST, chain_b, 0)
+    lon_states(z_plane, fin_b, 1, 1)
     for delta in range(1, LON):
-        lon_copy(lonc_b, delta, 1).start()
+        lon_copy(1, 1, delta).start()
+    lax.fori_loop(FIRST, CHUNKS, chain_b, 0)
+    lon_states(z_plane, fin_b, 1, 0)
+    for delta in range(1, LON):
+        lon_copy(1, 0, delta).start()
 
     def inside_b(y, carry):
         planes[y] = dot3(halves(planes[y]), (kb_hi[y], kb_lo[y]), ((1,), (0,)))
@@ -461,54 +498,60 @@
 
     lax.fori_loop(0, ROWS, inside_b, 0)
     load_r.wait()
-    for delta in range(1, LON):
-        lon_copy(lonc_b, delta, 1).wait_recv()
-    lon_incoming(lonc_b)
-
     sums = [jnp.zeros((8, COLS), F32)] * 4
-
-    def fold(x):
-        return jnp.sum(x.reshape(FIELDS // 8, 8, COLS), axis=0)
-
-    for y in range(ROWS):
-        at = pl.ds(y, FIELDS, stride=ROWS)
-        d, r = dvm[at, :], rvm[at, :]
-        h = d + (planes[y] + enter(y, ent_b))
-        nat[at, :] = h
-        sums = [sums[0] + fold(r * r), sums[1] + fold(d * h), sums[2] + fold(r * h), sums[3] + fold(h * h)]
-    store = pltpu.make_async_copy(nat, hess_out, out_sem.at[0])
-    store.start()
+    stores = []
+    for g in (1, 0):
+        first, count = GROUPS[g]
+        lon_incoming(1, g)
+        for y in range(ROWS):
+            at = pl.ds(first * ROWS + y, count, stride=ROWS)
+            d, r = dvm[at, :], rvm[at, :]
+            h = d + (z_plane(y, first, count) + enter(y, ent_b, g))
+            nat[at, :] = h
+            for k, product in enumerate((r * r, d * h, r * h, h * h)):
+                sums[k] = sums[k] + jnp.sum(product.reshape(count // 8, 8, COLS), axis=0)
+        part = pl.ds(first * ROWS, count * ROWS)
+        stores.append(pltpu.make_async_copy(nat.at[part], hess_out.at[part], out_sem.at[g]))
+        stores[-1].start()
 
     for k in range(4):
         tile[pl.ds(k, 1), :] = jnp.sum(sums[k], axis=0, keepdims=True)
     tile[pl.ds(4, 4), :] = jnp.zeros((4, COLS), F32)
 
-    def reduce(axis, me, count, slots, s_sem, r_sem):
+    def reduce(slots, me, s_sem, r_sem, peers):
         slots[me] = tile[...]
 
-        def copy(delta):
-            return pltpu.make_async_remote_copy(
-                src_ref=slots.at[me],
-                dst_ref=slots.at[me],
-                send_sem=s_sem.at[delta - 1],
-                recv_sem=r_sem.at[delta - 1],
-                device_id={axis: lax.rem(me + delta, count)},
-                device_id_type=MESH,
-            )
-
-        for delta in range(1, count):
-            copy(delta).start()
-        for delta in range(1, count):
-            copy(delta).wait_recv()
+        def copies():
+            for k, peer in enumerate(peers):
+                yield pltpu.make_async_remote_copy(
+                    src_ref=slots.at[me],
+                    dst_ref=slots.at[me],
+                    send_sem=s_sem.at[k],
+                    recv_sem=r_sem.at[k],
+                    device_id=peer,
+                    device_id_type=MESH,
+                )
+
+        for copy in copies():
+            copy.start()
+        for copy in copies():
+            copy.wait_recv()
         total = slots[0]
-        for k in range(1, count):
+        for k in range(1, len(peers) + 1):
             total = total + slots[k]
         tile[...] = total
-        return copy
-
-    copy_a = reduce("lon", me_lon, LON, red_a, ra_s, ra_r)
-    copy_b = reduce("mem", me_mem, MEM, red_b, rb_s, rb_r)
-    copy_c = reduce("lat", me_lat, LAT, red_c, rc_s, rc_r)
+        return copies
+
+    left_a = reduce(
+        red_a, me_mem * LON + me_lon, ra_s, ra_r,
+        [
+            {"lon": lax.rem(me_lon + dx, LON), "mem": lax.rem(me_mem + dy, MEM)}
+            for dy in range(MEM) for dx in range(LON) if dx or dy
+        ],
+    )
+    left_c = reduce(
+        red_c, me_lat, rc_s, rc_r, [{"lat": lax.rem(me_lat + dz, LAT)} for dz in range(1, LAT)]
+    )
     sums = jnp.broadcast_to(jnp.sum(tile[...], axis=1, keepdims=True), (8, COLS))
     rr, dh, rh, hh = (sums[k : k + 1] for k in range(4))
     step = rr / dh
@@ -516,17 +559,17 @@
     step_out[0, 0] = step[0, 0]
     ratio_out[0, 0] = (norm_new / rr)[0, 0]
 
-    store.wait()
-    for delta in range(1, LON):
-        lon_copy(lonc_f, delta, 0).wait_send()
-        lon_copy(lonc_b, delta, 1).wait_send()
-        copy_a(delta).wait_send()
+    for store in stores:
+        store.wait()
+    for phase in range(2):
+        for g in range(2):
+            for delta in range(1, LON):
+                lon_copy(phase, g, delta).wait_send()
     for delta in range(1, MEM):
         mem_copy(delta).wait_send()
-        copy_b(delta).wait_send()
-    for delta in range(1, LAT):
-        copy_c(delta).wait_send()
-
+    for left in (left_a, left_c):
+        for copy in left():
+            copy.wait_send()
     lat_left(lat_f, 0, p_f)
     lat_left(lat_b, 1, p_b)
 
@@ -535,11 +578,11 @@
     rows = FIELDS * ROWS
     any_space = pl.BlockSpec(memory_space=pl.ANY)
     smem = pl.BlockSpec(memory_space=pltpu.SMEM)
-    vmem = pl.BlockSpec(memory_space=pltpu.VMEM)
     dma = pltpu.SemaphoreType.DMA
     states = pltpu.VMEM((5, CHUNKS, 4, CHUNK, COLS), F32)
     table = pltpu.VMEM((ROWS, COLS, COLS), BF16)
-    slots = pltpu.VMEM((LON * STATES, FIELDS), F32)
+    slots = [pltpu.VMEM((LON * STATES, count), F32) for first, count in GROUPS]
+    mix = pltpu.VMEM((STATES, LON * STATES), BF16)
     small = pltpu.VMEM((STATES, COLS), F32)
     one = jax.ShapeDtypeStruct((1, 1), F32)
     hessian, step, ratio = pl.pallas_call(
@@ -549,9 +592,13 @@
             jax.ShapeDtypeStruct((rows, COLS), F32),
             one, one,
         ),
-        in_specs=[any_space, any_space, any_space, smem, smem, smem, vmem, any_space],
+        in_specs=[any_space] * 8,
         out_specs=(any_space, smem, smem),
         scratch_shapes=[
+            pltpu.SMEM(vert_modes.shape, F32),
+            pltpu.SMEM(eig_count.shape, jnp.int32),
+            pltpu.SMEM(lon_decay.shape, F32),
+            pltpu.VMEM((1, COLS), F32),
             pltpu.VMEM((rows, COLS), F32),
             pltpu.VMEM((rows, COLS), F32),
             pltpu.VMEM((FIELDS // MODES, LEVELS * ROWS, COLS), BF16),
@@ -560,22 +607,21 @@
             pltpu.VMEM((ROWS, FIELDS, COLS), F32),
             table, table, table, table,
             pltpu.VMEM((LEVELS * MODES, 8, COLS), F32),
-            slots, slots,
-            pltpu.VMEM((FIELDS, STATES), F32),
+            *slots, *slots,
+            *[pltpu.VMEM((count, STATES), F32) for first, count in GROUPS],
+            mix, mix,
             small, small, small, small,
             states, states,
             pltpu.VMEM((MEM, LEVELS * ROWS, COLS), F32),
             pltpu.VMEM((LEVELS * ROWS, COLS), F32),
-            pltpu.VMEM((LON, 8, COLS), F32),
-            pltpu.VMEM((MEM, 8, COLS), F32),
+            pltpu.VMEM((LON * MEM, 8, COLS), F32),
             pltpu.VMEM((LAT, 8, COLS), F32),
             pltpu.VMEM((8, COLS), F32),
-            dma((4,)), dma((1,)),
-            dma((2, LON - 1)), dma((2, LON - 1)),
+            dma((8,)), dma((2,)),
+            dma((2, 2, LON - 1)), dma((2, 2, LON - 1)),
             dma((2, 2, CHUNKS)), dma((2, 2, CHUNKS)),
             dma((MEM - 1,)), dma((MEM - 1,)),
-            dma((LON - 1,)), dma((LON - 1,)),
-            dma((MEM - 1,)), dma((MEM - 1,)),
+            dma((LON * MEM - 1,)), dma((LON * MEM - 1,)),
             dma((LAT - 1,)), dma((LAT - 1,)),
         ],
         compiler_params=pltpu.CompilerParams(

time: 90.7 us -> 81.3 us (0.90)
  Pallas kernels: 86.1 us -> 76.8 us
    pallas_call x1, Pallas kernels: 86.1 us -> 76.8 us  [body(): pl.pallas_call(kernel, name='cg_step', out_shape=(jax.ShapeDtypeStruct((r...]
where the time goes in v3:
time: 81.3 us; the launch traced here: 81.2 us
  Pallas kernels  76.8 us (94%)
  other arithmetic  3.75 us (5%)
    pallas_call x1, Pallas kernels, body(): pl.pallas_call(kernel, name='cg_step', out_shape=(jax.ShapeDtypeStruct((r...  76.8 us
    add x1, other arithmetic, body(): new_direction = new_residual + ratio * direction  3.75 us

profile of v3, /device:TPU:1, one launch (start us, length us, event | category | flops | bytes accessed | tf_op | source)
XLA Modules:
  0.0 81.2 jit_solution(94693173019449897)
XLA Ops:
  0.6 0.0 copy-start
  0.6 0.0 copy-start.1
  0.7 0.0 copy-start.2
  0.7 76.8 %cg_step.1 = (f32[1280,128]{1,0:T(8,128)}, f32[1,1]{1,0:T(1,128)}, f32[1,1]{1,0:T(1,128)}) custom-call(f32[1280,128]{1,0:T(8,128)} %bitcast.10, f32[1280,128]{1,0:T(8,128)} %bitcast.11, bf16[20,256,128]{2,1,0:T(8,128)(2,1)} %bitcast.12, f32[8,32]{1,0:T(8,128)} %vert_modes_in.1, s32[20]{0:T(128)} %eig_count_in.1, f32[8]{0:T(128)} %lon_decay_in.1, ...), custom_call_target="tpu_custom_call" | custom-call | tf_op jit(solution)/shard_map/cg_step/pallas_call | solution.py:588
  77.4 0.0 copy-done
  77.4 0.0 copy-done.1
  77.4 0.0 copy-done.2
  77.5 3.8 %multiply_add_fusion = (f32[160,8,128]{2,1,0:T(8,128)}, f32[160,8,128]{2,1,0:T(8,128)}, f32[160,8,128]{2,1,0:T(8,128)}) fusion(f32[160,8,128]{2,1,0:T(8,128)S(1)} %copy-done, f32[]{:T(128)} %bitcast.7, f32[160,8,128]{2,1,0:T(8,128)S(1)} %copy-done.1, f32[1280,128]{1,0:T(8,128)} %get-tuple-element.7, f32[]{:T(128)} %bitcast.5, f32[160,8,128]{2,1,0:T(8,128)S(1)} %copy-done.2), kind=kLoop, calls=%fused_computation.1 | loop fusion | flops 983040 | bytes 4587528 | tf_op jit(solution)/shard_map/add | solution.py:644
Async XLA Ops:
  0.6 76.8 %copy-start = (f32[160,8,128]{2,1,0:T(8,128)S(1)}, f32[160,8,128]{2,1,0:T(8,128)}, u32[]{:S(2)}) copy-start(f32[160,8,128]{2,1,0:T(8,128)} %param.11) | copy-start | bytes 1966084
  0.6 76.8 %copy-start.1 = (f32[160,8,128]{2,1,0:T(8,128)S(1)}, f32[160,8,128]{2,1,0:T(8,128)}, u32[]{:S(2)}) copy-start(f32[160,8,128]{2,1,0:T(8,128)} %param.10) | copy-start | bytes 1966084
  0.7 76.8 %copy-start.2 = (f32[160,8,128]{2,1,0:T(8,128)S(1)}, f32[160,8,128]{2,1,0:T(8,128)}, u32[]{:S(2)}) copy-start(f32[160,8,128]{2,1,0:T(8,128)} %param.9) | copy-start | bytes 1966084

commit v4 on v3

--- a/solution.py
+++ b/solution.py
@@ -16,7 +16,7 @@
 LEVELS, MODES = 32, 8
 CHUNK = 8
 GROUP = 2
-LAG = 12
+LAG = 10
 CHUNKS = FIELDS // CHUNK
 GROUPS = ((128, 32), (0, 128))
 FIRST = 16
@@ -45,6 +45,10 @@
 def dot3(a, b, dims):
     dot = functools.partial(lax.dot_general, dimension_numbers=(dims, ((), ())), preferred_element_type=F32)
     return dot(a[0], b[0]) + (dot(a[0], b[1]) + dot(a[1], b[0]))
+
+
+def far_first(count):
+    return sorted(range(1, count), key=lambda d: -min(d, count - d))
 
 
 def iota(shape, dim):
@@ -76,7 +80,7 @@
 
     barrier = pltpu.get_barrier_semaphore()
     for axis, me, count in (("lon", me_lon, LON), ("lat", me_lat, LAT), ("mem", me_mem, MEM)):
-        for delta in (1, LAT - 1) if axis == "lat" else range(1, count):
+        for delta in (1, LAT - 1) if axis == "lat" else far_first(count):
             pl.semaphore_signal(
                 barrier, inc=1, device_id={axis: lax.rem(me + delta, count)}, device_id_type=MESH
             )
@@ -209,7 +213,7 @@
     lon_states(d_plane, fin_f, 0, 1)
     pl.semaphore_wait(barrier, LON - 1 + 2 + MEM - 1)
     for g in range(2):
-        for delta in range(1, LON):
+        for delta in far_first(LON):
             lon_copy(0, g, delta).start()
 
     def inside_f(y, carry):
@@ -434,7 +438,7 @@
             device_id_type=MESH,
         )
 
-    for delta in range(1, MEM):
+    for delta in far_first(MEM):
         mem_copy(delta).start()
     load_o.wait()
     for delta in range(1, MEM):
@@ -485,11 +489,11 @@
 
     lax.fori_loop(0, FIRST, chain_b, 0)
     lon_states(z_plane, fin_b, 1, 1)
-    for delta in range(1, LON):
+    for delta in far_first(LON):
         lon_copy(1, 1, delta).start()
     lax.fori_loop(FIRST, CHUNKS, chain_b, 0)
     lon_states(z_plane, fin_b, 1, 0)
-    for delta in range(1, LON):
+    for delta in far_first(LON):
         lon_copy(1, 0, delta).start()
 
     def inside_b(y, carry):
@@ -518,7 +522,7 @@
         tile[pl.ds(k, 1), :] = jnp.sum(sums[k], axis=0, keepdims=True)
     tile[pl.ds(4, 4), :] = jnp.zeros((4, COLS), F32)
 
-    def reduce(slots, me, s_sem, r_sem, peers):
+    def reduce(slots, me, s_sem, r_sem, peers, meanwhile):
         slots[me] = tile[...]
 
         def copies():
@@ -534,6 +538,7 @@
 
         for copy in copies():
             copy.start()
+        meanwhile()
         for copy in copies():
             copy.wait_recv()
         total = slots[0]
@@ -542,15 +547,36 @@
         tile[...] = total
         return copies
 
+    def departed():
+        for store in stores:
+            store.wait()
+        for phase in range(2):
+            for g in range(2):
+                for delta in range(1, LON):
+                    lon_copy(phase, g, delta).wait_send()
+        for delta in range(1, MEM):
+            mem_copy(delta).wait_send()
+        lat_left(lat_f, 0, p_f)
+        lat_left(lat_b, 1, p_b)
+
+    def departed_a():
+        for copy in left_a():
+            copy.wait_send()
+
     left_a = reduce(
         red_a, me_mem * LON + me_lon, ra_s, ra_r,
         [
             {"lon": lax.rem(me_lon + dx, LON), "mem": lax.rem(me_mem + dy, MEM)}
-            for dy in range(MEM) for dx in range(LON) if dx or dy
+            for dx, dy in sorted(
+                [(dx, dy) for dy in range(MEM) for dx in range(LON) if dx or dy],
+                key=lambda d: -(min(d[1], MEM - d[1]) + min(d[0], LON - d[0]) / 2),
+            )
         ],
+        departed,
     )
     left_c = reduce(
-        red_c, me_lat, rc_s, rc_r, [{"lat": lax.rem(me_lat + dz, LAT)} for dz in range(1, LAT)]
+        red_c, me_lat, rc_s, rc_r, [{"lat": lax.rem(me_lat + dz, LAT)} for dz in far_first(LAT)],
+        departed_a,
     )
     sums = jnp.broadcast_to(jnp.sum(tile[...], axis=1, keepdims=True), (8, COLS))
     rr, dh, rh, hh = (sums[k : k + 1] for k in range(4))
@@ -559,19 +585,8 @@
     step_out[0, 0] = step[0, 0]
     ratio_out[0, 0] = (norm_new / rr)[0, 0]
 
-    for store in stores:
-        store.wait()
-    for phase in range(2):
-        for g in range(2):
-            for delta in range(1, LON):
-                lon_copy(phase, g, delta).wait_send()
-    for delta in range(1, MEM):
-        mem_copy(delta).wait_send()
-    for left in (left_a, left_c):
-        for copy in left():
-            copy.wait_send()
-    lat_left(lat_f, 0, p_f)
-    lat_left(lat_b, 1, p_b)
+    for copy in left_c():
+        copy.wait_send()
 
 
 def body(control, residual, direction, members, vert_modes, eig_count, lon_decay, lat_decay, obs_weight):

time: 81.3 us -> 80 us (0.984)
  Pallas kernels: 76.8 us -> 75.4 us
    pallas_call x1, Pallas kernels: 76.8 us -> 75.4 us  [body(): pl.pallas_call(kernel, name='cg_step', out_shape=(jax.ShapeDtypeStruct((r...]
where the time goes in v4:
time: 80 us; the launch traced here: 79.9 us
  Pallas kernels  75.4 us (94%)
  other arithmetic  3.75 us (5%)
    pallas_call x1, Pallas kernels, body(): pl.pallas_call(kernel, name='cg_step', out_shape=(jax.ShapeDtypeStruct((r...  75.4 us
    add x1, other arithmetic, body(): new_direction = new_residual + ratio * direction  3.75 us

profile of v4, /device:TPU:1, one launch (start us, length us, event | category | flops | bytes accessed | tf_op | source)
XLA Modules:
  0.0 79.9 jit_solution(1355990400962451950)
XLA Ops:
  0.6 0.0 copy-start
  0.6 0.0 copy-start.1
  0.7 0.0 copy-start.2
  0.7 75.4 %cg_step.1 = (f32[1280,128]{1,0:T(8,128)}, f32[1,1]{1,0:T(1,128)}, f32[1,1]{1,0:T(1,128)}) custom-call(f32[1280,128]{1,0:T(8,128)} %bitcast.10, f32[1280,128]{1,0:T(8,128)} %bitcast.11, bf16[20,256,128]{2,1,0:T(8,128)(2,1)} %bitcast.12, f32[8,32]{1,0:T(8,128)} %vert_modes_in.1, s32[20]{0:T(128)} %eig_count_in.1, f32[8]{0:T(128)} %lon_decay_in.1, ...), custom_call_target="tpu_custom_call" | custom-call | tf_op jit(solution)/shard_map/cg_step/pallas_call | solution.py:603
  76.1 0.0 copy-done
  76.1 0.0 copy-done.1
  76.1 0.0 copy-done.2
  76.1 3.8 %multiply_add_fusion = (f32[160,8,128]{2,1,0:T(8,128)}, f32[160,8,128]{2,1,0:T(8,128)}, f32[160,8,128]{2,1,0:T(8,128)}) fusion(f32[160,8,128]{2,1,0:T(8,128)S(1)} %copy-done, f32[]{:T(128)} %bitcast.7, f32[160,8,128]{2,1,0:T(8,128)S(1)} %copy-done.1, f32[1280,128]{1,0:T(8,128)} %get-tuple-element.7, f32[]{:T(128)} %bitcast.5, f32[160,8,128]{2,1,0:T(8,128)S(1)} %copy-done.2), kind=kLoop, calls=%fused_computation.1 | loop fusion | flops 983040 | bytes 4587528 | tf_op jit(solution)/shard_map/add | solution.py:659
Async XLA Ops:
  0.6 75.5 %copy-start = (f32[160,8,128]{2,1,0:T(8,128)S(1)}, f32[160,8,128]{2,1,0:T(8,128)}, u32[]{:S(2)}) copy-start(f32[160,8,128]{2,1,0:T(8,128)} %param.11) | copy-start | bytes 1966084
  0.6 75.5 %copy-start.1 = (f32[160,8,128]{2,1,0:T(8,128)S(1)}, f32[160,8,128]{2,1,0:T(8,128)}, u32[]{:S(2)}) copy-start(f32[160,8,128]{2,1,0:T(8,128)} %param.10) | copy-start | bytes 1966084
  0.7 75.5 %copy-start.2 = (f32[160,8,128]{2,1,0:T(8,128)S(1)}, f32[160,8,128]{2,1,0:T(8,128)}, u32[]{:S(2)}) copy-start(f32[160,8,128]{2,1,0:T(8,128)} %param.9) | copy-start | bytes 1966084

commit v5 on v4

--- a/solution.py
+++ b/solution.py
@@ -16,7 +16,7 @@
 LEVELS, MODES = 32, 8
 CHUNK = 8
 GROUP = 2
-LAG = 10
+LAG = 9
 CHUNKS = FIELDS // CHUNK
 GROUPS = ((128, 32), (0, 128))
 FIRST = 16

time: 80 us -> 79.2 us (0.990)
  Pallas kernels: 75.4 us -> 74.6 us
    pallas_call x1, Pallas kernels: 75.4 us -> 74.6 us  [body(): pl.pallas_call(kernel, name='cg_step', out_shape=(jax.ShapeDtypeStruct((r...]
where the time goes in v5:
time: 79.2 us; the launch traced here: 79.1 us
  Pallas kernels  74.6 us (94%)
  other arithmetic  3.75 us (5%)
    pallas_call x1, Pallas kernels, body(): pl.pallas_call(kernel, name='cg_step', out_shape=(jax.ShapeDtypeStruct((r...  74.6 us
    add x1, other arithmetic, body(): new_direction = new_residual + ratio * direction  3.75 us

profile of v5, /device:TPU:1, one launch (start us, length us, event | category | flops | bytes accessed | tf_op | source)
XLA Modules:
  0.0 79.1 jit_solution(7570539795900195216)
XLA Ops:
  0.6 0.0 copy-start
  0.6 0.0 copy-start.1
  0.7 0.0 copy-start.2
  0.7 74.6 %cg_step.1 = (f32[1280,128]{1,0:T(8,128)}, f32[1,1]{1,0:T(1,128)}, f32[1,1]{1,0:T(1,128)}) custom-call(f32[1280,128]{1,0:T(8,128)} %bitcast.10, f32[1280,128]{1,0:T(8,128)} %bitcast.11, bf16[20,256,128]{2,1,0:T(8,128)(2,1)} %bitcast.12, f32[8,32]{1,0:T(8,128)} %vert_modes_in.1, s32[20]{0:T(128)} %eig_count_in.1, f32[8]{0:T(128)} %lon_decay_in.1, ...), custom_call_target="tpu_custom_call" | custom-call | tf_op jit(solution)/shard_map/cg_step/pallas_call | solution.py:603
  75.3 0.0 copy-done
  75.3 0.0 copy-done.1
  75.3 0.0 copy-done.2
  75.3 3.8 %multiply_add_fusion = (f32[160,8,128]{2,1,0:T(8,128)}, f32[160,8,128]{2,1,0:T(8,128)}, f32[160,8,128]{2,1,0:T(8,128)}) fusion(f32[160,8,128]{2,1,0:T(8,128)S(1)} %copy-done, f32[]{:T(128)} %bitcast.7, f32[160,8,128]{2,1,0:T(8,128)S(1)} %copy-done.1, f32[1280,128]{1,0:T(8,128)} %get-tuple-element.7, f32[]{:T(128)} %bitcast.5, f32[160,8,128]{2,1,0:T(8,128)S(1)} %copy-done.2), kind=kLoop, calls=%fused_computation.1 | loop fusion | flops 983040 | bytes 4587528 | tf_op jit(solution)/shard_map/add | solution.py:659
Async XLA Ops:
  0.6 74.7 %copy-start = (f32[160,8,128]{2,1,0:T(8,128)S(1)}, f32[160,8,128]{2,1,0:T(8,128)}, u32[]{:S(2)}) copy-start(f32[160,8,128]{2,1,0:T(8,128)} %param.11) | copy-start | bytes 1966084
  0.6 74.7 %copy-start.1 = (f32[160,8,128]{2,1,0:T(8,128)S(1)}, f32[160,8,128]{2,1,0:T(8,128)}, u32[]{:S(2)}) copy-start(f32[160,8,128]{2,1,0:T(8,128)} %param.10) | copy-start | bytes 1966084
  0.7 74.7 %copy-start.2 = (f32[160,8,128]{2,1,0:T(8,128)S(1)}, f32[160,8,128]{2,1,0:T(8,128)}, u32[]{:S(2)}) copy-start(f32[160,8,128]{2,1,0:T(8,128)} %param.9) | copy-start | bytes 1966084
